TPU v7x, 256 devices: a whole 4x4x8 slice. The times are simulated.
256 devices in a mesh: row: 16 (over z_lo, y), col: 16 (over z_hi, x, core).
Axes of the slice: x: 4, y: 4, z: 8 (z_hi: 2, z_lo: 4; z = z_hi * 4 + z_lo), core: 2. Of those that a mesh axis runs over, the one named last changes fastest.
Arguments:
- amplitudes_right: float32 [8, 16384], P(None, ('row', 'col')), may hold values from -5 to 5
- amplitudes_left: float32 [8, 16384], P(None, ('row', 'col')), may hold values from -7 to 7
- previous_right: float32 [8, 16384], P(None, ('row', 'col')), may hold values from -6 to 6
- previous_left: float32 [8, 16384], P(None, ('row', 'col')), may hold values from -6 to 6
- coupling: float32 [2, 8], replicated, may hold values from 0.2 to 1
- ladder: bfloat16 [16384, 16384], P('row', 'col'), may hold values from -1 to 5
Outputs:
- next_right: float32 [8, 16384], P(None, ('row', 'col'))
- next_left: float32 [8, 16384], P(None, ('row', 'col'))
- coefficients: float32 [3, 8], replicated
All inputs are finite; a program needn't handle non-finite values.
Results may differ from a plain program's by a relative error of at most 0.003.
Values may be sent and summed in bfloat16 or wider, within the bound.
No kernel may reach another device: no remote copies, remote signals or barrier semaphores. Data moves between devices by JAX's collectives and lax.ppermute only.
A program may use at most 64 MiB of HBM per device.

v0:
```python
import jax
import jax.numpy as jnp
from jax import lax
from jax.sharding import PartitionSpec as P


def broadcast(array, axis, root):
    mine = lax.axis_index(axis) == root
    return lax.psum(jnp.where(mine, array, jnp.zeros_like(array)), axis)


def local(amplitudes_right, amplitudes_left, previous_right, previous_left, coupling, ladder):
    rows_count = lax.axis_size("row")
    cols_count = lax.axis_size("col")
    my_row = lax.axis_index("row")
    my_col = lax.axis_index("col")
    share = amplitudes_right.shape[1]
    pairs_total = share * rows_count * cols_count
    block_cols = ladder.shape[1]
    stride_factor = rows_count // cols_count
    right_half = amplitudes_right.astype(jnp.bfloat16)
    left_half = amplitudes_left.astype(jnp.bfloat16)
    whole_right = lax.all_gather(right_half, ("row", "col"), axis=1, tiled=True)
    column_block = lax.dynamic_slice_in_dim(whole_right, my_col * block_cols, block_cols, 1)
    right_terms = lax.dot_general(
        column_block, ladder, (((1,), (1,)), ((), ())), preferred_element_type=jnp.float32
    )
    image_right = lax.psum_scatter(right_terms, "col", scatter_dimension=1, tiled=True)
    left_terms = jnp.dot(
        lax.all_gather(left_half, "col", axis=1, tiled=True),
        ladder,
        preferred_element_type=jnp.float32,
    )
    column_sum = lax.psum(left_terms, "row")
    donor_col = my_row // stride_factor
    relayed_left = broadcast(column_sum, "col", donor_col)
    offset = my_row % stride_factor * cols_count + my_col
    image_left = lax.dynamic_slice_in_dim(relayed_left, offset * share, share, 1)
    gamma_old = coupling[1]
    beta_old = coupling[0]
    alpha_now = (
        lax.psum(jnp.sum(amplitudes_left * image_right, axis=1), ("row", "col")) / pairs_total
    )
    right_res = (
        image_right - alpha_now[:, None] * amplitudes_right - gamma_old[:, None] * previous_right
    )
    left_res = image_left - alpha_now[:, None] * amplitudes_left - beta_old[:, None] * previous_left
    omega_sum, right_sum, left_sum = lax.psum(
        (
            jnp.sum(left_res * right_res, axis=1),
            jnp.sum(right_res * right_res, axis=1),
            jnp.sum(left_res * left_res, axis=1),
        ),
        ("row", "col"),
    )
    omega_val = omega_sum / pairs_total
    right_norm = right_sum / pairs_total
    left_norm = left_sum / pairs_total
    safe_omega = jnp.maximum(jnp.abs(omega_val), 0.1 * jnp.sqrt(right_norm * left_norm + 1e-06))
    beta_new = jnp.sqrt(safe_omega)
    gamma_new = omega_val / beta_new
    next_right = right_res / beta_new[:, None]
    next_left = left_res * (gamma_new / safe_omega)[:, None]
    coefficients = jnp.stack([alpha_now, beta_new, gamma_new])
    return (next_right, next_left, coefficients)


def solution(mesh):
    placed = (
        P(None, ("row", "col")),
        P(None, ("row", "col")),
        P(None, ("row", "col")),
        P(None, ("row", "col")),
        P(),
        P("row", "col"),
    )
    return jax.shard_map(
        local,
        mesh=mesh,
        in_specs=placed,
        out_specs=(P(None, ("row", "col")), P(None, ("row", "col")), P()),
        check_vma=False,
    )
```

profile of v0, /device:TPU:1, one launch (start us, length us, event | category | flops | bytes accessed | tf_op | source)
XLA Modules:
  0.0 832.5 jit_solution(6970357341052498828)
XLA Ops:
  7.2 0.0 copy-start
  7.2 0.0 reduce-scatter.4.cloned.1.call-start
  7.2 0.8 convert_bitcast_fusion.1
  8.1 378.0 %all-gather = bf16[256,64,8]{1,2,0:T(8,128)(2,1)S(1)} all-gather(bf16[1,64,8]{1,2,0:T(8,128)(2,1)S(1)} %convert_bitcast_fusion.1), channel_id=1, replica_groups=mesh['row'=16,'col'=16] {'row','col'}, dimensions={0}, use_global_device_ids=true | all-gather | bytes 263168 | tf_op jit(solution)/shard_map/all_gather | solution.py:23
  386.0 0.1 copy.11
  386.1 0.0 copy-start.5
  386.1 0.0 copy-start.1
  386.1 0.5 reshape.12
  386.6 0.0 copy-done
  386.6 1.5 convolution_bitcast_fusion
  388.1 0.0 copy-start.2
  388.1 0.0 copy-start.3
  388.1 0.0 copy-start.4
  388.1 0.0 reduce-scatter.4.cloned.1.call-update
  388.1 0.0 copy-done.5
  388.1 99.4 %reduce-scatter.4.cloned.1.call-done = f32[64,8]{1,0:T(8,128)} async-done(((f32[1024,8]{1,0:T(8,128)}), f32[64,8]{1,0:T(8,128)}) %reduce-scatter.4.cloned.1.call-update) | async-done | bytes 2064
  487.5 0.8 copy.14
  488.3 0.0 copy-done.1
  488.3 0.1 convert_bitcast_fusion
  488.4 75.8 %psum.42 = f32[8]{0:T(128)S(1)} all-reduce(f32[8]{0:T(128)S(1)} %get-tuple-element.14), channel_id=1, replica_groups=mesh['row'=16,'col'=16] {'row','col'}, use_global_device_ids=true, to_apply=%region_2.3 | all-reduce | flops 8 | bytes 64 | tf_op jit(solution)/shard_map/psum | solution.py:42
  564.3 28.1 %all-gather.1 = bf16[16,64,8]{1,2,0:T(8,128)(2,1)S(1)} all-gather(bf16[1,64,8]{1,2,0:T(8,128)(2,1)S(1)} %get-tuple-element.13), channel_id=1, replica_groups=mesh['row'=16,'col'=16] {'col'}, dimensions={0}, use_global_device_ids=true | all-gather | bytes 17408 | tf_op jit(solution)/shard_map/all_gather | solution.py:30
  592.4 0.1 reshape.14
  592.5 0.4 fusion.3
  592.9 62.3 %psum.43 = f32[8,1024]{1,0:T(8,128)S(1)} all-reduce(f32[8,1024]{1,0:T(8,128)S(1)} %fusion.3), channel_id=1, replica_groups=mesh['row'=16,'col'=16] {'row'}, use_global_device_ids=true, to_apply=%region_3.4 | all-reduce | flops 8192 | bytes 65536 | tf_op jit(solution)/shard_map/psum | solution.py:34
  655.2 90.2 %psum.44 = f32[8,1024]{1,0:T(8,128)S(1)} all-reduce(f32[8,1024]{1,0:T(8,128)S(1)} %broadcast_select_fusion), channel_id=1, replica_groups=mesh['row'=16,'col'=16] {'col'}, use_global_device_ids=true, to_apply=%region_4.5 | all-reduce | flops 8192 | bytes 65536 | tf_op jit(solution)/shard_map/psum | solution.py:9
  745.3 0.0 copy-done.2
  745.3 0.0 copy-done.3
  745.3 0.0 copy-done.4
  745.3 0.2 multiply_reduce_fusion.2
  745.6 78.8 %all-reduce = (f32[8]{0:T(128)S(1)}, f32[8]{0:T(128)S(1)}, f32[8]{0:T(128)S(1)}) all-reduce(f32[8]{0:T(128)S(1)} %get-tuple-element.5, f32[8]{0:T(128)S(1)} %get-tuple-element.4, f32[8]{0:T(128)S(1)} %get-tuple-element.3), channel_id=1, replica_groups=mesh['row'=16,'col'=16] {'row','col'}, use_global_device_ids=true, to_apply=%region_10.11 | all-reduce | flops 24 | bytes 192 | tf_op jit(solution)/shard_map/psum | solution.py:48
  824.4 0.6 pad_maximum_fusion
  825.0 0.7 broadcast_multiply_fusion
  (6 shorter events, 0.0 us)
Async XLA Ops:
  7.2 379.4 %copy-start = (bf16[1024,1024]{1,0:T(8,128)(2,1)S(1)}, bf16[1024,1024]{1,0:T(8,128)(2,1)}, u32[]{:S(2)}) copy-start(bf16[1024,1024]{1,0:T(8,128)(2,1)} %param.11) | copy-start | bytes 6291460
  7.2 480.3 %reduce-scatter.4.cloned.1.call-start = ((), (), s32[]{:S(2)}) async-start(), calls=%async_computation.1 | async-start | bytes 557056
  386.1 2.0 copy-start.5
  386.1 102.2 %copy-start.1 = (f32[8,64]{1,0:T(8,128)S(1)}, f32[8,64]{1,0:T(8,128)}, u32[]{:S(2)}) copy-start(f32[8,64]{1,0:T(8,128)} %param.7) | copy-start | bytes 6148
  388.1 357.3 %copy-start.2 = (f32[8,64]{1,0:T(8,128)S(1)}, f32[8,64]{1,0:T(8,128)}, u32[]{:S(2)}) copy-start(f32[8,64]{1,0:T(8,128)} %param.6) | copy-start | bytes 6148
  388.1 357.3 %copy-start.3 = (f32[8,64]{1,0:T(8,128)S(1)}, f32[8,64]{1,0:T(8,128)}, u32[]{:S(2)}) copy-start(f32[8,64]{1,0:T(8,128)} %param.9) | copy-start | bytes 6148
  388.1 357.3 %copy-start.4 = (f32[8,64]{1,0:T(8,128)S(1)}, f32[8,64]{1,0:T(8,128)}, u32[]{:S(2)}) copy-start(f32[8,64]{1,0:T(8,128)} %param.8) | copy-start | bytes 6148
Sparse Core Ops, SparseCore 0:
  388.2 99.2 reduce-scatter.3
where the time goes:
time: 833 us
  blocking collectives  713 us (86%)
  waiting for transfers between devices  99.4 us (12%)
  between operations  14.1 us (2%)
    all_gather x1, blocking collectives, local(): whole_right = lax.all_gather(right_half, ('row', 'col'), axis=1, tiled=True)  378 us
    unnamed x2, waiting for transfers between devices  99.4 us
    psum x1, blocking collectives, broadcast(): return lax.psum(jnp.where(mine, array, jnp.zeros_like(array)), axis)  90.2 us
    psum x1, blocking collectives, local(): lax.psum((jnp.sum(left_res * right_res, axis=1), jnp.sum(right_res * righ...  78.8 us
    psum x1, blocking collectives, local(): lax.psum(jnp.sum(amplitudes_left * image_right, axis=1), ('row', 'col'))  75.8 us
    psum x1, blocking collectives, local(): column_sum = lax.psum(left_terms, 'row')  62.3 us
    all_gather x1, blocking collectives, local(): lax.all_gather(left_half, 'col', axis=1, tiled=True)  28.1 us
  transfers between devices with their start and end apart: 1, of which 1 were waited for; matrix products, arithmetic and copies ran while one was open for 0% of the time, Pallas kernels for 0%

commit v1 on v0

v1 whole, which is shorter than its diff:
```python
import functools

import jax
import jax.numpy as jnp
from jax import lax
from jax.experimental import pallas as pl
from jax.experimental.pallas import tpu as pltpu
from jax.sharding import PartitionSpec as P

AXES = ("row", "col")
HALF = 64
LANES = 128
SLOTS = 16
CANCEL = 1e-3
VMEM = pl.BlockSpec(memory_space=pltpu.VMEM)
PARAMS = pltpu.CompilerParams(vmem_limit_bytes=32 * 1024 * 1024)


def lane_of(shape):
    return lax.broadcasted_iota(jnp.int32, shape, 1)


def sublane_of(shape):
    return lax.broadcasted_iota(jnp.int32, shape, 0)


def swap(tile):
    return pltpu.roll(tile, HALF, 1)


def column_of(row):
    wide = jnp.broadcast_to(row, (8, 8))
    return jnp.sum(jnp.where(lane_of((8, 8)) == sublane_of((8, 8)), wide, 0.0), axis=1, keepdims=True)


def pack_kernel(right, left, prev_right, prev_left, coupling, chunks, both, damped):
    tile = jnp.concatenate([right[...], left[...]], axis=1)
    both[...] = tile
    chunks[...] = jnp.broadcast_to(tile[None], chunks.shape)
    damped[...] = jnp.concatenate(
        [
            column_of(coupling[1:2, :]) * prev_right[...],
            column_of(coupling[0:1, :]) * prev_left[...],
        ],
        axis=1,
    )


def left_kernel(gathered, ladder, out):
    low = lane_of((8, LANES)) < HALF
    pieces = []
    for m in range(gathered.shape[0] // 2):
        pieces.append(jnp.where(low, swap(gathered[2 * m]), gathered[2 * m + 1]))
    block = jnp.concatenate(pieces, axis=1).astype(jnp.bfloat16)
    terms = jnp.dot(block, ladder[...], preferred_element_type=jnp.float32)
    for m in range(gathered.shape[0] // 2):
        piece = terms[:, LANES * m : LANES * (m + 1)]
        out[2 * m] = jnp.where(low, gathered[2 * m], swap(piece))
        out[2 * m + 1] = jnp.where(low, gathered[2 * m + 1], piece)


def right_kernel(turned, ladder, out):
    low = lane_of((8, LANES)) < HALF
    pieces = []
    for m in range(turned.shape[0] // 2):
        pieces.append(jnp.where(low, turned[2 * m], swap(turned[2 * m + 1])))
    block = jnp.concatenate(pieces, axis=1).astype(jnp.bfloat16)
    terms = lax.dot_general(
        block, ladder[...], (((1,), (1,)), ((), ())), preferred_element_type=jnp.float32
    )
    for m in range(turned.shape[0] // 2):
        piece = terms[:, LANES * m : LANES * (m + 1)]
        out[2 * m] = jnp.where(low, piece, turned[2 * m])
        out[2 * m + 1] = jnp.where(low, swap(piece), turned[2 * m + 1])


def products_kernel(partials, both, damped, rows, reduced):
    shape = (8, LANES)
    lane = lane_of(shape)
    low = lane < HALF
    image = jnp.sum(partials[...], axis=0)
    pair = both[...]
    crossed = swap(pair)
    work = image - damped[...]
    reduced[...] = work

    def total(tile):
        return jnp.sum(tile, axis=1, keepdims=True)

    def lower(tile):
        return total(jnp.where(low, tile, 0.0))

    def upper(tile):
        return total(jnp.where(low, 0.0, tile))

    own = work * pair
    square = work * work
    base = pair * pair
    dots = (
        lower(image * crossed),
        lower(work * swap(work)),
        total(work * crossed),
        lower(pair * crossed),
        lower(square),
        lower(own),
        lower(base),
        upper(square),
        upper(own),
        upper(base),
    )
    slot = lane % SLOTS
    table = jnp.zeros(shape, jnp.float32)
    for at, dot in enumerate(dots):
        table = jnp.where(slot == at, dot, table)
    row = jnp.sum(jnp.where(lane // SLOTS == sublane_of(shape), table, 0.0), axis=0, keepdims=True)
    rows[...] = jnp.broadcast_to(row, rows.shape)


def finish_kernel(pairs_total, rows, reduced, both, next_right, next_left, coefficients, flag):
    shape = (8, LANES)
    lane = lane_of(shape)
    row = jnp.sum(rows[...], axis=0, keepdims=True) / pairs_total
    table = jnp.where(lane // SLOTS == sublane_of(shape), jnp.broadcast_to(row, shape), 0.0)
    dots = [
        jnp.sum(jnp.where(lane % SLOTS == at, table, 0.0), axis=1, keepdims=True)
        for at in range(10)
    ]
    alpha = dots[0]
    omega = dots[1] - alpha * dots[2] + alpha * alpha * dots[3]
    right_norm = dots[4] - 2.0 * alpha * dots[5] + alpha * alpha * dots[6]
    left_norm = dots[7] - 2.0 * alpha * dots[8] + alpha * alpha * dots[9]
    right_safe = right_norm - CANCEL * (dots[4] + alpha * alpha * dots[6])
    left_safe = left_norm - CANCEL * (dots[7] + alpha * alpha * dots[9])
    weak = jnp.where(jnp.minimum(right_safe, left_safe) > 0.0, 0.0, 1.0)
    flag[0, 0] = jnp.max(weak).astype(jnp.int32)
    safe = jnp.maximum(
        jnp.abs(omega),
        0.1 * jnp.sqrt(jnp.maximum(right_norm, 0.0) * jnp.maximum(left_norm, 0.0) + 1e-6),
    )
    beta = jnp.sqrt(safe)
    gamma = omega / beta
    residual = reduced[...] - alpha * both[...]
    scaled = residual * jnp.where(lane < HALF, 1.0 / beta, gamma / safe)
    next_right[...] = scaled[:, :HALF]
    next_left[...] = scaled[:, HALF:]
    diagonal = lane == sublane_of(shape)
    for at, value in enumerate((alpha, beta, gamma)):
        line = jnp.sum(jnp.where(diagonal, value, 0.0), axis=0, keepdims=True)
        coefficients[at : at + 1, :] = line[:, :8]


def direct(pairs_total, reduced, both, coefficients):
    alpha = coefficients[0]
    residual = reduced - alpha[:, None] * both
    right_res, left_res = residual[:, :HALF], residual[:, HALF:]
    sums = jnp.stack(
        [
            jnp.sum(left_res * right_res, axis=1),
            jnp.sum(right_res * right_res, axis=1),
            jnp.sum(left_res * left_res, axis=1),
        ]
    )
    omega, right_norm, left_norm = lax.psum(sums, AXES) / pairs_total
    safe = jnp.maximum(jnp.abs(omega), 0.1 * jnp.sqrt(right_norm * left_norm + 1e-6))
    beta = jnp.sqrt(safe)
    gamma = omega / beta
    next_right = right_res / beta[:, None]
    next_left = left_res * (gamma / safe)[:, None]
    return next_right, next_left, jnp.stack([alpha, beta, gamma])


def local(amplitudes_right, amplitudes_left, previous_right, previous_left, coupling, ladder):
    count = lax.axis_size("col")
    devices = lax.axis_size("row") * count
    pairs_total = amplitudes_right.shape[1] * devices
    wide = jax.ShapeDtypeStruct((count, 8, LANES), jnp.float32)
    tile = jax.ShapeDtypeStruct((8, LANES), jnp.float32)
    ladder = pltpu.with_memory_space_constraint(ladder, pltpu.VMEM)

    with jax.named_scope("pack"):
        chunks, both, damped = pl.pallas_call(
            pack_kernel, out_shape=(wide, tile, tile), in_specs=[VMEM] * 5,
            out_specs=(VMEM,) * 3, compiler_params=PARAMS,
        )(amplitudes_right, amplitudes_left, previous_right, previous_left, coupling)
    gathered = lax.all_to_all(chunks, "col", 0, 0, tiled=True)
    with jax.named_scope("left_product"):
        packed = pl.pallas_call(
            left_kernel, out_shape=wide, in_specs=[VMEM] * 2, out_specs=VMEM,
            compiler_params=PARAMS,
        )(gathered, ladder)
    transpose = [(i * count + j, j * count + i) for i in range(count) for j in range(count)]
    turned = lax.ppermute(packed, AXES, transpose)
    with jax.named_scope("right_product"):
        partials = pl.pallas_call(
            right_kernel, out_shape=wide, in_specs=[VMEM] * 2, out_specs=VMEM,
            compiler_params=PARAMS,
        )(turned, ladder)
    partials = lax.all_to_all(partials, "col", 0, 0, tiled=True)
    with jax.named_scope("inner_products"):
        rows, reduced = pl.pallas_call(
            products_kernel,
            out_shape=(jax.ShapeDtypeStruct((devices, LANES), jnp.float32), tile),
            in_specs=[VMEM] * 3, out_specs=(VMEM,) * 2, compiler_params=PARAMS,
        )(partials, both, damped)
    rows = lax.all_to_all(rows, AXES, 0, 0, tiled=True)
    half = jax.ShapeDtypeStruct((8, HALF), jnp.float32)
    with jax.named_scope("finish"):
        next_right, next_left, coefficients, flag = pl.pallas_call(
            functools.partial(finish_kernel, float(pairs_total)),
            out_shape=(
                half, half, jax.ShapeDtypeStruct((3, 8), jnp.float32),
                jax.ShapeDtypeStruct((1, 1), jnp.int32),
            ),
            in_specs=[VMEM] * 3,
            out_specs=(VMEM,) * 3 + (pl.BlockSpec(memory_space=pltpu.SMEM),),
            compiler_params=PARAMS,
        )(rows, reduced, both)
    return lax.cond(
        flag[0, 0] > 0,
        lambda: direct(float(pairs_total), reduced, both, coefficients),
        lambda: (next_right, next_left, coefficients),
    )


def solution(mesh):
    placed = (
        P(None, AXES),
        P(None, AXES),
        P(None, AXES),
        P(None, AXES),
        P(),
        P("row", "col"),
    )
    return jax.shard_map(
        local,
        mesh=mesh,
        in_specs=placed,
        out_specs=(P(None, AXES), P(None, AXES), P()),
        check_vma=False,
    )
```

time: 833 us -> 78.6 us (0.09)
  blocking collectives: 713 us -> 62.2 us
  waiting for transfers between devices: 99.4 us -> 2.05 us
  between operations: 14.1 us -> 1.34 us
    all_gather x2 -> x0, blocking collectives: 406 us -> none  [the longest x1 378 us: local(): whole_right = lax.all_gather(right_half, ('row', 'col'), axis=1, tiled=True)]
    psum x4 -> x0, blocking collectives: 307 us -> none  [the longest x1 90.2 us: broadcast(): return lax.psum(jnp.where(mine, array, jnp.zeros_like(array)), axis)]
    unnamed x2 -> x0, waiting for transfers between devices: 99.4 us -> none
    all_to_all x0 -> x3, blocking collectives: none -> 62.2 us  [the longest x1 22 us: local(): gathered = lax.all_to_all(chunks, 'col', 0, 0, tiled=True)]
where the time goes in v1:
time: 78.6 us; the launch traced here: 78.2 us
  blocking collectives  62.2 us (79%)
  local copies, waits for them, and re-layouts  6.77 us (9%)
  starting transfers between devices  3.66 us (5%)
  Pallas kernels  2.21 us (3%)
  waiting for transfers between devices  2.05 us (3%)
  between operations  1.34 us (2%)
    all_to_all x1, blocking collectives, local(): gathered = lax.all_to_all(chunks, 'col', 0, 0, tiled=True)  22 us
    all_to_all x1, blocking collectives, local(): partials = lax.all_to_all(partials, 'col', 0, 0, tiled=True)  21.1 us
    all_to_all x1, blocking collectives, local(): rows = lax.all_to_all(rows, AXES, 0, 0, tiled=True)  19.2 us
    unnamed x20, local copies, waits for them, and re-layouts  6.77 us
    ppermute x1, starting transfers between devices, local(): turned = lax.ppermute(packed, AXES, transpose)  3.66 us
    ppermute x1, waiting for transfers between devices, local(): turned = lax.ppermute(packed, AXES, transpose)  2.05 us
  transfers between devices with their start and end apart: 1, of which 1 were waited for; matrix products, arithmetic and copies ran while one was open for 0% of the time, Pallas kernels for 0%

profile of v1, /device:TPU:1, one launch (start us, length us, event | category | flops | bytes accessed | tf_op | source)
XLA Modules:
  0.0 78.2 jit_solution(16519593868010645355)
XLA Ops:
  0.6 0.0 copy-start.2
  0.6 0.7 copy-done.2
  1.3 0.0 copy-start.3
  1.3 0.7 copy-done.3
  2.0 0.0 copy-start.4
  2.0 0.7 copy-done.4
  2.7 0.0 copy-start.5
  2.7 0.7 copy-done.5
  3.4 0.0 copy-start.6
  3.4 0.7 copy-done.6
  4.1 0.1 pack.1
  4.2 22.0 %all_to_all.21.gathered = f32[16,8,128]{2,1,0:T(8,128)S(1)} all-to-all(f32[16,8,128]{2,1,0:T(8,128)S(1)} %get-tuple-element.27), channel_id=1, replica_groups=mesh['row'=16,'col'=16] {'col'}, dimensions={0} | all-to-all | bytes 131072 | tf_op jit(solution)/shard_map/all_to_all | solution.py:185
  26.2 0.0 copy-start
  26.2 1.6 %copy-done = bf16[1024,1024]{1,0:T(8,128)(2,1)S(1)} copy-done((bf16[1024,1024]{1,0:T(8,128)(2,1)S(1)}, bf16[1024,1024]{1,0:T(8,128)(2,1)}, u32[]{:S(2)}) %copy-start) | copy-done | bytes 2097176
  27.8 0.0 copy-start.1
  27.8 0.5 left_product.1
  28.2 3.7 %collective-permute-start = (f32[16,8,128]{2,1,0:T(8,128)S(1)}, f32[16,8,128]{2,1,0:T(8,128)S(1)}, u32[]{:S(2)}, u32[]{:S(2)}) collective-permute-start(f32[16,8,128]{2,1,0:T(8,128)S(1)} %left_product.1), channel_id=1, source_target_pairs={{0,0},{1,16},{2,32},{3,48},{4,64},{5,80},{6,96},{7,112},{8,128},{9... | collective-permute-start | bytes 196616 | tf_op jit(solution)/shard_map/ppermute | solution.py:192
  31.9 2.0 %collective-permute-done.turned = f32[16,8,128]{2,1,0:T(8,128)S(1)} collective-permute-done((f32[16,8,128]{2,1,0:T(8,128)S(1)}, f32[16,8,128]{2,1,0:T(8,128)S(1)}, u32[]{:S(2)}, u32[]{:S(2)}) %collective-permute-start) | collective-permute-done | bytes 65568 | tf_op jit(solution)/shard_map/ppermute | solution.py:192
  34.0 0.0 copy-done.1
  34.0 0.7 right_product.1
  34.7 21.1 %all_to_all.22.partials = f32[16,8,128]{2,1,0:T(8,128)S(1)} all-to-all(f32[16,8,128]{2,1,0:T(8,128)S(1)} %right_product.1), channel_id=1, replica_groups=mesh['row'=16,'col'=16] {'col'}, dimensions={0} | all-to-all | bytes 131072 | tf_op jit(solution)/shard_map/all_to_all | solution.py:198
  55.7 0.2 inner_products.1
  55.9 19.2 %all_to_all.23 = f32[256,1,128]{2,1,0:T(1,128)S(1)} all-to-all(f32[256,1,128]{2,1,0:T(1,128)S(1)} %bitcast.26), channel_id=1, replica_groups=mesh['row'=16,'col'=16] {'row','col'}, dimensions={0} | all-to-all | bytes 262144 | tf_op jit(solution)/shard_map/all_to_all | solution.py:205
  75.1 0.7 finish.1
  76.5 0.0 copy-start.7
  76.5 0.6 copy-done.7
  77.1 0.0 copy-start.8
  77.1 0.6 copy-done.8
  77.7 0.0 copy-start.9
  77.7 0.6 copy-done.9
  (1 shorter events, 0.0 us)
Async XLA Ops:
  0.6 0.7 copy-start.2
  1.3 0.7 copy-start.3
  2.0 0.7 copy-start.4
  2.7 0.7 copy-start.5
  3.4 0.7 copy-start.6
  26.2 1.6 %copy-start = (bf16[1024,1024]{1,0:T(8,128)(2,1)S(1)}, bf16[1024,1024]{1,0:T(8,128)(2,1)}, u32[]{:S(2)}) copy-start(bf16[1024,1024]{1,0:T(8,128)(2,1)} %ladder.3) | copy-start | bytes 6291460
  27.8 6.2 %copy-start.1 = (bf16[1024,1024]{1,0:T(8,128)(2,1)S(1)}, bf16[1024,1024]{1,0:T(8,128)(2,1)}, u32[]{:S(2)}) copy-start(bf16[1024,1024]{1,0:T(8,128)(2,1)} %ladder.3) | copy-start | bytes 6291460
  28.2 5.7 %collective-permute-start = (f32[16,8,128]{2,1,0:T(8,128)S(1)}, f32[16,8,128]{2,1,0:T(8,128)S(1)}, u32[]{:S(2)}, u32[]{:S(2)}) collective-permute-start(f32[16,8,128]{2,1,0:T(8,128)S(1)} %left_product.1), channel_id=1, source_target_pairs={{0,0},{1,16},{2,32},{3,48},{4,64},{5,80},{6,96},{7,112},{8,128},{9... | collective-permute-start | bytes 196616 | tf_op jit(solution)/shard_map/ppermute | solution.py:192
  76.5 0.6 copy-start.7
  77.1 0.6 copy-start.8
  77.7 0.6 copy-start.9

commit v2 on v1

--- a/solution.py
+++ b/solution.py
@@ -10,9 +10,9 @@
 AXES = ("row", "col")
 HALF = 64
 LANES = 128
-SLOTS = 16
 CANCEL = 1e-3
 VMEM = pl.BlockSpec(memory_space=pltpu.VMEM)
+HBM = pl.BlockSpec(memory_space=pltpu.HBM)
 PARAMS = pltpu.CompilerParams(vmem_limit_bytes=32 * 1024 * 1024)
 
 
@@ -33,20 +33,25 @@
     return jnp.sum(jnp.where(lane_of((8, 8)) == sublane_of((8, 8)), wide, 0.0), axis=1, keepdims=True)
 
 
-def pack_kernel(right, left, prev_right, prev_left, coupling, chunks, both, damped):
-    tile = jnp.concatenate([right[...], left[...]], axis=1)
+def fetch(sources, targets, sems):
+    copies = [
+        pltpu.make_async_copy(source, target, sems.at[at])
+        for at, (source, target) in enumerate(zip(sources, targets, strict=True))
+    ]
+    for copy in copies:
+        copy.start()
+    return copies
+
+
+def pack_kernel(right, left, chunks, both, right_here, left_here, sems):
+    for copy in fetch((right, left), (right_here, left_here), sems):
+        copy.wait()
+    tile = jnp.concatenate([right_here[...], left_here[...]], axis=1)
     both[...] = tile
     chunks[...] = jnp.broadcast_to(tile[None], chunks.shape)
-    damped[...] = jnp.concatenate(
-        [
-            column_of(coupling[1:2, :]) * prev_right[...],
-            column_of(coupling[0:1, :]) * prev_left[...],
-        ],
-        axis=1,
-    )
-
-
-def left_kernel(gathered, ladder, out):
+
+
+def left_kernel(gathered, ladder, prev_right, prev_left, coupling, out, damped):
     low = lane_of((8, LANES)) < HALF
     pieces = []
     for m in range(gathered.shape[0] // 2):
@@ -57,6 +62,13 @@
         piece = terms[:, LANES * m : LANES * (m + 1)]
         out[2 * m] = jnp.where(low, gathered[2 * m], swap(piece))
         out[2 * m + 1] = jnp.where(low, gathered[2 * m + 1], piece)
+    damped[...] = jnp.concatenate(
+        [
+            column_of(coupling[1:2, :]) * prev_right[...],
+            column_of(coupling[0:1, :]) * prev_left[...],
+        ],
+        axis=1,
+    )
 
 
 def right_kernel(turned, ladder, out):
@@ -108,30 +120,32 @@
         upper(own),
         upper(base),
     )
-    slot = lane % SLOTS
+    slot = lane // 8
     table = jnp.zeros(shape, jnp.float32)
     for at, dot in enumerate(dots):
         table = jnp.where(slot == at, dot, table)
-    row = jnp.sum(jnp.where(lane // SLOTS == sublane_of(shape), table, 0.0), axis=0, keepdims=True)
+    row = jnp.sum(jnp.where(lane % 8 == sublane_of(shape), table, 0.0), axis=0, keepdims=True)
     rows[...] = jnp.broadcast_to(row, rows.shape)
 
 
-def finish_kernel(pairs_total, rows, reduced, both, next_right, next_left, coefficients, flag):
+def finish_kernel(
+    pairs_total, rows, reduced, both,
+    next_right, next_left, coefficients, flag, right_here, left_here, coefficients_here, sems,
+):
     shape = (8, LANES)
     lane = lane_of(shape)
-    row = jnp.sum(rows[...], axis=0, keepdims=True) / pairs_total
-    table = jnp.where(lane // SLOTS == sublane_of(shape), jnp.broadcast_to(row, shape), 0.0)
-    dots = [
-        jnp.sum(jnp.where(lane % SLOTS == at, table, 0.0), axis=1, keepdims=True)
-        for at in range(10)
-    ]
+    row = jnp.sum(rows[...], axis=0, keepdims=True) * (1.0 / pairs_total)
+    wide = jnp.broadcast_to(row, shape)
+    dots = [wide] + [pltpu.roll(wide, LANES - 8 * at, 1) for at in range(1, 10)]
     alpha = dots[0]
-    omega = dots[1] - alpha * dots[2] + alpha * alpha * dots[3]
-    right_norm = dots[4] - 2.0 * alpha * dots[5] + alpha * alpha * dots[6]
-    left_norm = dots[7] - 2.0 * alpha * dots[8] + alpha * alpha * dots[9]
-    right_safe = right_norm - CANCEL * (dots[4] + alpha * alpha * dots[6])
-    left_safe = left_norm - CANCEL * (dots[7] + alpha * alpha * dots[9])
-    weak = jnp.where(jnp.minimum(right_safe, left_safe) > 0.0, 0.0, 1.0)
+    square = alpha * alpha
+    omega = dots[1] - alpha * dots[2] + square * dots[3]
+    right_norm = dots[4] - 2.0 * alpha * dots[5] + square * dots[6]
+    left_norm = dots[7] - 2.0 * alpha * dots[8] + square * dots[9]
+    right_safe = right_norm - CANCEL * (dots[4] + square * dots[6])
+    left_safe = left_norm - CANCEL * (dots[7] + square * dots[9])
+    strong = jnp.minimum(right_safe, left_safe) > 0.0
+    weak = jnp.where(jnp.logical_or(strong, lane >= 8), 0.0, 1.0)
     flag[0, 0] = jnp.max(weak).astype(jnp.int32)
     safe = jnp.maximum(
         jnp.abs(omega),
@@ -139,14 +153,20 @@
     )
     beta = jnp.sqrt(safe)
     gamma = omega / beta
-    residual = reduced[...] - alpha * both[...]
-    scaled = residual * jnp.where(lane < HALF, 1.0 / beta, gamma / safe)
-    next_right[...] = scaled[:, :HALF]
-    next_left[...] = scaled[:, HALF:]
     diagonal = lane == sublane_of(shape)
+
+    def column(value):
+        return jnp.sum(jnp.where(diagonal, value, 0.0), axis=1, keepdims=True)
+
+    residual = reduced[...] - column(alpha) * both[...]
+    scaled = residual * jnp.where(lane < HALF, column(1.0 / beta), column(gamma / safe))
+    right_here[...] = scaled[:, :HALF]
+    left_here[...] = scaled[:, HALF:]
     for at, value in enumerate((alpha, beta, gamma)):
-        line = jnp.sum(jnp.where(diagonal, value, 0.0), axis=0, keepdims=True)
-        coefficients[at : at + 1, :] = line[:, :8]
+        coefficients_here[at : at + 1, :] = value[:1, :8]
+    targets = (next_right, next_left, coefficients)
+    for copy in fetch((right_here, left_here, coefficients_here), targets, sems):
+        copy.wait()
 
 
 def direct(pairs_total, reduced, both, coefficients):
@@ -177,17 +197,22 @@
     tile = jax.ShapeDtypeStruct((8, LANES), jnp.float32)
     ladder = pltpu.with_memory_space_constraint(ladder, pltpu.VMEM)
 
+    half = pltpu.VMEM((8, HALF), jnp.float32)
+    stay = functools.partial(pltpu.with_memory_space_constraint, memory_space=pltpu.HBM)
     with jax.named_scope("pack"):
-        chunks, both, damped = pl.pallas_call(
-            pack_kernel, out_shape=(wide, tile, tile), in_specs=[VMEM] * 5,
-            out_specs=(VMEM,) * 3, compiler_params=PARAMS,
-        )(amplitudes_right, amplitudes_left, previous_right, previous_left, coupling)
+        chunks, both = pl.pallas_call(
+            pack_kernel, out_shape=(wide, tile), in_specs=[HBM] * 2, out_specs=(VMEM,) * 2,
+            scratch_shapes=[half, half, pltpu.SemaphoreType.DMA((2,))],
+            cost_estimate=pl.CostEstimate(flops=10_000_000_000, bytes_accessed=65_536, transcendentals=0),
+            compiler_params=PARAMS,
+        )(stay(amplitudes_right), stay(amplitudes_left))
     gathered = lax.all_to_all(chunks, "col", 0, 0, tiled=True)
     with jax.named_scope("left_product"):
-        packed = pl.pallas_call(
-            left_kernel, out_shape=wide, in_specs=[VMEM] * 2, out_specs=VMEM,
-            compiler_params=PARAMS,
-        )(gathered, ladder)
+        packed, damped = pl.pallas_call(
+            left_kernel, out_shape=(wide, tile), in_specs=[VMEM] * 5,
+            out_specs=(VMEM,) * 2,
+            compiler_params=PARAMS,
+        )(gathered, ladder, previous_right, previous_left, coupling)
     transpose = [(i * count + j, j * count + i) for i in range(count) for j in range(count)]
     turned = lax.ppermute(packed, AXES, transpose)
     with jax.named_scope("right_product"):
@@ -203,16 +228,19 @@
             in_specs=[VMEM] * 3, out_specs=(VMEM,) * 2, compiler_params=PARAMS,
         )(partials, both, damped)
     rows = lax.all_to_all(rows, AXES, 0, 0, tiled=True)
-    half = jax.ShapeDtypeStruct((8, HALF), jnp.float32)
+    half_out = pltpu.HBM((8, HALF), jnp.float32)
     with jax.named_scope("finish"):
         next_right, next_left, coefficients, flag = pl.pallas_call(
             functools.partial(finish_kernel, float(pairs_total)),
             out_shape=(
-                half, half, jax.ShapeDtypeStruct((3, 8), jnp.float32),
-                jax.ShapeDtypeStruct((1, 1), jnp.int32),
+                half_out, half_out, pltpu.HBM((3, 8), jnp.float32),
+                pltpu.SMEM((1, 1), jnp.int32),
             ),
             in_specs=[VMEM] * 3,
-            out_specs=(VMEM,) * 3 + (pl.BlockSpec(memory_space=pltpu.SMEM),),
+            out_specs=(HBM,) * 3 + (pl.BlockSpec(memory_space=pltpu.SMEM),),
+            scratch_shapes=[
+                half, half, pltpu.VMEM((3, 8), jnp.float32), pltpu.SemaphoreType.DMA((3,)),
+            ],
             compiler_params=PARAMS,
         )(rows, reduced, both)
     return lax.cond(

time: 78.6 us -> 72 us (0.916)
  local copies, waits for them, and re-layouts: 6.77 us -> 0.02 us
  Pallas kernels: 2.21 us -> 3.22 us
    unnamed x20 -> x8, local copies, waits for them, and re-layouts: 6.77 us -> 0.02 us
    pallas_call x2, Pallas kernels: 0.63 us -> 1.43 us  [the longest x1 0.94 us: local(): pl.pallas_call(pack_kernel, out_shape=(wide, tile), in_specs=[HBM] * 2, o...]
where the time goes in v2:
time: 72 us; the launch traced here: 71.8 us
  blocking collectives  62.2 us (86%)
  starting transfers between devices  3.53 us (5%)
  Pallas kernels  3.22 us (4%)
  waiting for transfers between devices  2.05 us (3%)
  between operations  0.72 us (1%)
    all_to_all x1, blocking collectives, local(): gathered = lax.all_to_all(chunks, 'col', 0, 0, tiled=True)  22 us
    all_to_all x1, blocking collectives, local(): partials = lax.all_to_all(partials, 'col', 0, 0, tiled=True)  21.1 us
    all_to_all x1, blocking collectives, local(): rows = lax.all_to_all(rows, AXES, 0, 0, tiled=True)  19.2 us
    ppermute x1, starting transfers between devices, local(): turned = lax.ppermute(packed, AXES, transpose)  3.53 us
    ppermute x1, waiting for transfers between devices, local(): turned = lax.ppermute(packed, AXES, transpose)  2.05 us
  transfers between devices with their start and end apart: 1, of which 1 were waited for; matrix products, arithmetic and copies ran while one was open for 0% of the time, Pallas kernels for 0%

profile of v2, /device:TPU:1, one launch (start us, length us, event | category | flops | bytes accessed | tf_op | source)
XLA Modules:
  0.0 71.8 jit_solution(10818594197397120708)
XLA Ops:
  0.6 0.0 copy-start
  0.6 0.0 copy-start.3
  0.7 0.0 copy-start.2
  0.7 0.0 copy-start.1
  0.7 0.9 %pack.1 = (f32[16,8,128]{2,1,0:T(8,128)S(1)}, f32[8,128]{1,0:T(8,128)S(1)}) custom-call(f32[8,64]{1,0:T(8,128)} %right.1, f32[8,64]{1,0:T(8,128)} %left.1), custom_call_target="tpu_custom_call" | custom-call | flops 10000000000 | bytes 65536 | tf_op jit(solution)/shard_map/pack/pallas_call | solution.py:203
  1.6 22.0 %all_to_all.21.gathered = f32[16,8,128]{2,1,0:T(8,128)S(1)} all-to-all(f32[16,8,128]{2,1,0:T(8,128)S(1)} %get-tuple-element.28), channel_id=1, replica_groups=mesh['row'=16,'col'=16] {'col'}, dimensions={0} | all-to-all | bytes 131072 | tf_op jit(solution)/shard_map/all_to_all | solution.py:209
  23.6 0.0 copy-done
  23.6 0.0 copy-done.3
  23.6 0.0 copy-done.2
  23.6 0.0 copy-done.1
  23.6 0.5 left_product.1
  24.1 3.5 %collective-permute-start = (f32[16,8,128]{2,1,0:T(8,128)S(1)}, f32[16,8,128]{2,1,0:T(8,128)S(1)}, u32[]{:S(2)}, u32[]{:S(2)}) collective-permute-start(f32[16,8,128]{2,1,0:T(8,128)S(1)} %get-tuple-element.29), channel_id=1, source_target_pairs={{0,0},{1,16},{2,32},{3,48},{4,64},{5,80},{6,96},{7,112},{8,128},{9... | collective-permute-start | bytes 196616 | tf_op jit(solution)/shard_map/ppermute | solution.py:217
  27.6 2.0 %collective-permute-done.turned = f32[16,8,128]{2,1,0:T(8,128)S(1)} collective-permute-done((f32[16,8,128]{2,1,0:T(8,128)S(1)}, f32[16,8,128]{2,1,0:T(8,128)S(1)}, u32[]{:S(2)}, u32[]{:S(2)}) %collective-permute-start) | collective-permute-done | bytes 65568 | tf_op jit(solution)/shard_map/ppermute | solution.py:217
  29.7 0.7 right_product.1
  30.4 21.1 %all_to_all.22.partials = f32[16,8,128]{2,1,0:T(8,128)S(1)} all-to-all(f32[16,8,128]{2,1,0:T(8,128)S(1)} %right_product.1), channel_id=1, replica_groups=mesh['row'=16,'col'=16] {'col'}, dimensions={0} | all-to-all | bytes 131072 | tf_op jit(solution)/shard_map/all_to_all | solution.py:223
  51.4 0.2 inner_products.1
  51.6 19.2 %all_to_all.23 = f32[256,1,128]{2,1,0:T(1,128)S(1)} all-to-all(f32[256,1,128]{2,1,0:T(1,128)S(1)} %bitcast.26), channel_id=1, replica_groups=mesh['row'=16,'col'=16] {'row','col'}, dimensions={0} | all-to-all | bytes 262144 | tf_op jit(solution)/shard_map/all_to_all | solution.py:230
  70.8 0.9 %finish.1 = (f32[8,64]{1,0:T(8,128)}, f32[8,64]{1,0:T(8,128)}, f32[3,8]{1,0:T(4,128)}, s32[1,1]{1,0:T(1,128)S(4)}) custom-call(f32[256,128]{1,0:T(8,128)S(1)} %bitcast.25, f32[8,128]{1,0:T(8,128)S(1)} %get-tuple-element.33.reduced, f32[8,128]{1,0:T(8,128)S(1)} %get-tuple-element.30.both), custom_call_target="tpu_custom_call" | custom-call | tf_op jit(solution)/shard_map/finish/pallas_call | solution.py:233
  (1 shorter events, 0.0 us)
Async XLA Ops:
  0.6 23.0 %copy-start = (bf16[1024,1024]{1,0:T(8,128)(2,1)S(1)}, bf16[1024,1024]{1,0:T(8,128)(2,1)}, u32[]{:S(2)}) copy-start(bf16[1024,1024]{1,0:T(8,128)(2,1)} %ladder.3) | copy-start | bytes 6291460
  0.6 22.9 %copy-start.3 = (f32[2,8]{1,0:T(2,128)S(1)}, f32[2,8]{1,0:T(2,128)}, u32[]{:S(2)}) copy-start(f32[2,8]{1,0:T(2,128)} %coupling.1) | copy-start | bytes 196
  0.7 22.9 %copy-start.2 = (f32[8,64]{1,0:T(8,128)S(1)}, f32[8,64]{1,0:T(8,128)}, u32[]{:S(2)}) copy-start(f32[8,64]{1,0:T(8,128)} %prev_left.1) | copy-start | bytes 6148
  0.7 22.9 %copy-start.1 = (f32[8,64]{1,0:T(8,128)S(1)}, f32[8,64]{1,0:T(8,128)}, u32[]{:S(2)}) copy-start(f32[8,64]{1,0:T(8,128)} %prev_right.1) | copy-start | bytes 6148
  24.1 5.6 %collective-permute-start = (f32[16,8,128]{2,1,0:T(8,128)S(1)}, f32[16,8,128]{2,1,0:T(8,128)S(1)}, u32[]{:S(2)}, u32[]{:S(2)}) collective-permute-start(f32[16,8,128]{2,1,0:T(8,128)S(1)} %get-tuple-element.29), channel_id=1, source_target_pairs={{0,0},{1,16},{2,32},{3,48},{4,64},{5,80},{6,96},{7,112},{8,128},{9... | collective-permute-start | bytes 196616 | tf_op jit(solution)/shard_map/ppermute | solution.py:217

commit v3 on v2

--- a/solution.py
+++ b/solution.py
@@ -48,20 +48,24 @@
         copy.wait()
     tile = jnp.concatenate([right_here[...], left_here[...]], axis=1)
     both[...] = tile
-    chunks[...] = jnp.broadcast_to(tile[None], chunks.shape)
+    chunks[...] = jnp.broadcast_to(tile.astype(jnp.bfloat16)[None], chunks.shape)
 
 
 def left_kernel(gathered, ladder, prev_right, prev_left, coupling, out, damped):
     low = lane_of((8, LANES)) < HALF
-    pieces = []
+    rights, lefts = [], []
     for m in range(gathered.shape[0] // 2):
-        pieces.append(jnp.where(low, swap(gathered[2 * m]), gathered[2 * m + 1]))
-    block = jnp.concatenate(pieces, axis=1).astype(jnp.bfloat16)
+        even, odd = gathered[2 * m].astype(jnp.float32), gathered[2 * m + 1].astype(jnp.float32)
+        rights.append(jnp.where(low, even, swap(odd)))
+        lefts.append(jnp.where(low, swap(even), odd))
+    block = jnp.concatenate(lefts, axis=1).astype(jnp.bfloat16)
     terms = jnp.dot(block, ladder[...], preferred_element_type=jnp.float32)
-    for m in range(gathered.shape[0] // 2):
-        piece = terms[:, LANES * m : LANES * (m + 1)]
-        out[2 * m] = jnp.where(low, gathered[2 * m], swap(piece))
-        out[2 * m + 1] = jnp.where(low, gathered[2 * m + 1], piece)
+    high = terms.astype(jnp.bfloat16).astype(jnp.float32)
+    rest = terms - high
+    width = terms.shape[1]
+    upper = jnp.concatenate(rights + [rest[:, : width // 2]], axis=1)
+    lower = jnp.concatenate([high, rest[:, width // 2 :]], axis=1)
+    out[...] = jnp.concatenate([upper, lower], axis=0).astype(jnp.bfloat16)
     damped[...] = jnp.concatenate(
         [
             column_of(coupling[1:2, :]) * prev_right[...],
@@ -73,17 +77,21 @@
 
 def right_kernel(turned, ladder, out):
     low = lane_of((8, LANES)) < HALF
-    pieces = []
-    for m in range(turned.shape[0] // 2):
-        pieces.append(jnp.where(low, turned[2 * m], swap(turned[2 * m + 1])))
-    block = jnp.concatenate(pieces, axis=1).astype(jnp.bfloat16)
+    width = ladder.shape[1]
+    block = turned[:, :width][:8]
     terms = lax.dot_general(
         block, ladder[...], (((1,), (1,)), ((), ())), preferred_element_type=jnp.float32
     )
-    for m in range(turned.shape[0] // 2):
-        piece = terms[:, LANES * m : LANES * (m + 1)]
-        out[2 * m] = jnp.where(low, piece, turned[2 * m])
-        out[2 * m + 1] = jnp.where(low, swap(piece), turned[2 * m + 1])
+    for m in range(out.shape[0] // 2):
+        at = LANES * m
+        side = at % (width // 2)
+        half = 8 * (at // (width // 2))
+        high = turned[:, at : at + LANES].astype(jnp.float32)[8:]
+        rest = turned[:, width + side : width + side + LANES].astype(jnp.float32)[half : half + 8]
+        left = high + rest
+        piece = terms[:, at : at + LANES]
+        out[2 * m] = jnp.where(low, piece, swap(left))
+        out[2 * m + 1] = jnp.where(low, swap(piece), left)
 
 
 def products_kernel(partials, both, damped, rows, reduced):
@@ -142,11 +150,6 @@
     omega = dots[1] - alpha * dots[2] + square * dots[3]
     right_norm = dots[4] - 2.0 * alpha * dots[5] + square * dots[6]
     left_norm = dots[7] - 2.0 * alpha * dots[8] + square * dots[9]
-    right_safe = right_norm - CANCEL * (dots[4] + square * dots[6])
-    left_safe = left_norm - CANCEL * (dots[7] + square * dots[9])
-    strong = jnp.minimum(right_safe, left_safe) > 0.0
-    weak = jnp.where(jnp.logical_or(strong, lane >= 8), 0.0, 1.0)
-    flag[0, 0] = jnp.max(weak).astype(jnp.int32)
     safe = jnp.maximum(
         jnp.abs(omega),
         0.1 * jnp.sqrt(jnp.maximum(right_norm, 0.0) * jnp.maximum(left_norm, 0.0) + 1e-6),
@@ -165,7 +168,13 @@
     for at, value in enumerate((alpha, beta, gamma)):
         coefficients_here[at : at + 1, :] = value[:1, :8]
     targets = (next_right, next_left, coefficients)
-    for copy in fetch((right_here, left_here, coefficients_here), targets, sems):
+    copies = fetch((right_here, left_here, coefficients_here), targets, sems)
+    right_safe = right_norm - CANCEL * (dots[4] + square * dots[6])
+    left_safe = left_norm - CANCEL * (dots[7] + square * dots[9])
+    strong = jnp.minimum(right_safe, left_safe) > 0.0
+    weak = jnp.where(jnp.logical_or(strong, lane >= 8), 0.0, 1.0)
+    flag[0, 0] = jnp.max(weak).astype(jnp.int32)
+    for copy in copies:
         copy.wait()
 
 
@@ -194,6 +203,9 @@
     devices = lax.axis_size("row") * count
     pairs_total = amplitudes_right.shape[1] * devices
     wide = jax.ShapeDtypeStruct((count, 8, LANES), jnp.float32)
+    thin = jax.ShapeDtypeStruct((count, 8, LANES), jnp.bfloat16)
+    block = ladder.shape[1]
+    folded = jax.ShapeDtypeStruct((16, block + block // 2), jnp.bfloat16)
     tile = jax.ShapeDtypeStruct((8, LANES), jnp.float32)
     ladder = pltpu.with_memory_space_constraint(ladder, pltpu.VMEM)
 
@@ -201,7 +213,7 @@
     stay = functools.partial(pltpu.with_memory_space_constraint, memory_space=pltpu.HBM)
     with jax.named_scope("pack"):
         chunks, both = pl.pallas_call(
-            pack_kernel, out_shape=(wide, tile), in_specs=[HBM] * 2, out_specs=(VMEM,) * 2,
+            pack_kernel, out_shape=(thin, tile), in_specs=[HBM] * 2, out_specs=(VMEM,) * 2,
             scratch_shapes=[half, half, pltpu.SemaphoreType.DMA((2,))],
             cost_estimate=pl.CostEstimate(flops=10_000_000_000, bytes_accessed=65_536, transcendentals=0),
             compiler_params=PARAMS,
@@ -209,7 +221,7 @@
     gathered = lax.all_to_all(chunks, "col", 0, 0, tiled=True)
     with jax.named_scope("left_product"):
         packed, damped = pl.pallas_call(
-            left_kernel, out_shape=(wide, tile), in_specs=[VMEM] * 5,
+            left_kernel, out_shape=(folded, tile), in_specs=[VMEM] * 5,
             out_specs=(VMEM,) * 2,
             compiler_params=PARAMS,
         )(gathered, ladder, previous_right, previous_left, coupling)

time: 72 us -> 71.1 us (0.987)
    all_to_all x1, blocking collectives: 21.1 us -> 20.3 us  [local(): partials = lax.all_to_all(partials, 'col', 0, 0, tiled=True)]
where the time goes in v3:
time: 71.1 us; the launch traced here: 70.9 us
  blocking collectives  61.6 us (87%)
  starting transfers between devices  3.48 us (5%)
  Pallas kernels  3.16 us (4%)
  waiting for transfers between devices  1.92 us (3%)
  between operations  0.72 us (1%)
    all_to_all x1, blocking collectives, local(): gathered = lax.all_to_all(chunks, 'col', 0, 0, tiled=True)  21.9 us
    all_to_all x1, blocking collectives, local(): partials = lax.all_to_all(partials, 'col', 0, 0, tiled=True)  20.3 us
    all_to_all x1, blocking collectives, local(): rows = lax.all_to_all(rows, AXES, 0, 0, tiled=True)  19.4 us
    ppermute x1, starting transfers between devices, local(): turned = lax.ppermute(packed, AXES, transpose)  3.48 us
    ppermute x1, waiting for transfers between devices, local(): turned = lax.ppermute(packed, AXES, transpose)  1.92 us
  transfers between devices with their start and end apart: 1, of which 1 were waited for; matrix products, arithmetic and copies ran while one was open for 0% of the time, Pallas kernels for 0%

profile of v3, /device:TPU:1, one launch (start us, length us, event | category | flops | bytes accessed | tf_op | source)
XLA Modules:
  0.0 70.9 jit_solution(8261243408829966349)
XLA Ops:
  0.6 0.0 copy-start
  0.6 0.0 copy-start.3
  0.7 0.0 copy-start.2
  0.7 0.0 copy-start.1
  0.7 0.9 %pack.1 = (bf16[16,8,128]{2,1,0:T(8,128)(2,1)S(1)}, f32[8,128]{1,0:T(8,128)S(1)}) custom-call(f32[8,64]{1,0:T(8,128)} %right.1, f32[8,64]{1,0:T(8,128)} %left.1), custom_call_target="tpu_custom_call" | custom-call | flops 10000000000 | bytes 65536 | tf_op jit(solution)/shard_map/pack/pallas_call | solution.py:215
  1.6 21.9 %all_to_all.21.gathered = bf16[16,8,128]{2,1,0:T(8,128)(2,1)S(1)} all-to-all(bf16[16,8,128]{2,1,0:T(8,128)(2,1)S(1)} %get-tuple-element.28), channel_id=1, replica_groups=mesh['row'=16,'col'=16] {'col'}, dimensions={0} | all-to-all | bytes 65536 | tf_op jit(solution)/shard_map/all_to_all | solution.py:221
  23.6 0.0 copy-done
  23.6 0.0 copy-done.3
  23.6 0.0 copy-done.2
  23.6 0.0 copy-done.1
  23.6 0.4 left_product.1
  24.0 3.5 %collective-permute-start = (bf16[16,1536]{1,0:T(8,128)(2,1)S(1)}, bf16[16,1536]{1,0:T(8,128)(2,1)S(1)}, u32[]{:S(2)}, u32[]{:S(2)}) collective-permute-start(bf16[16,1536]{1,0:T(8,128)(2,1)S(1)} %get-tuple-element.29), channel_id=1, source_target_pairs={{0,0},{1,16},{2,32},{3,48},{4,64},{5,80},{6,96},{7,112},{8,128},{9... | collective-permute-start | bytes 147464 | tf_op jit(solution)/shard_map/ppermute | solution.py:229
  27.5 1.9 %collective-permute-done.turned = bf16[16,1536]{1,0:T(8,128)(2,1)S(1)} collective-permute-done((bf16[16,1536]{1,0:T(8,128)(2,1)S(1)}, bf16[16,1536]{1,0:T(8,128)(2,1)S(1)}, u32[]{:S(2)}, u32[]{:S(2)}) %collective-permute-start) | collective-permute-done | bytes 49184 | tf_op jit(solution)/shard_map/ppermute | solution.py:229
  29.4 0.7 %right_product.1 = f32[16,8,128]{2,1,0:T(8,128)S(1)} custom-call(bf16[16,1536]{1,0:T(8,128)(2,1)S(1)} %collective-permute-done.turned, bf16[1024,1024]{1,0:T(8,128)(2,1)S(1)} %copy-done), custom_call_target="tpu_custom_call" | custom-call | tf_op jit(solution)/shard_map/right_product/pallas_call | solution.py:231
  30.1 20.3 %all_to_all.22.partials = f32[16,8,128]{2,1,0:T(8,128)S(1)} all-to-all(f32[16,8,128]{2,1,0:T(8,128)S(1)} %right_product.1), channel_id=1, replica_groups=mesh['row'=16,'col'=16] {'col'}, dimensions={0} | all-to-all | bytes 131072 | tf_op jit(solution)/shard_map/all_to_all | solution.py:235
  50.4 0.2 inner_products.1
  50.6 19.4 %all_to_all.23 = f32[256,1,128]{2,1,0:T(1,128)S(1)} all-to-all(f32[256,1,128]{2,1,0:T(1,128)S(1)} %bitcast.26), channel_id=1, replica_groups=mesh['row'=16,'col'=16] {'row','col'}, dimensions={0} | all-to-all | bytes 262144 | tf_op jit(solution)/shard_map/all_to_all | solution.py:242
  70.0 0.9 %finish.1 = (f32[8,64]{1,0:T(8,128)}, f32[8,64]{1,0:T(8,128)}, f32[3,8]{1,0:T(4,128)}, s32[1,1]{1,0:T(1,128)S(4)}) custom-call(f32[256,128]{1,0:T(8,128)S(1)} %bitcast.25, f32[8,128]{1,0:T(8,128)S(1)} %get-tuple-element.33.reduced, f32[8,128]{1,0:T(8,128)S(1)} %get-tuple-element.30.both), custom_call_target="tpu_custom_call" | custom-call | tf_op jit(solution)/shard_map/finish/pallas_call | solution.py:245
  (1 shorter events, 0.0 us)
Async XLA Ops:
  0.6 22.9 %copy-start = (bf16[1024,1024]{1,0:T(8,128)(2,1)S(1)}, bf16[1024,1024]{1,0:T(8,128)(2,1)}, u32[]{:S(2)}) copy-start(bf16[1024,1024]{1,0:T(8,128)(2,1)} %ladder.3) | copy-start | bytes 6291460
  0.6 22.9 %copy-start.3 = (f32[2,8]{1,0:T(2,128)S(1)}, f32[2,8]{1,0:T(2,128)}, u32[]{:S(2)}) copy-start(f32[2,8]{1,0:T(2,128)} %coupling.1) | copy-start | bytes 196
  0.7 22.9 %copy-start.2 = (f32[8,64]{1,0:T(8,128)S(1)}, f32[8,64]{1,0:T(8,128)}, u32[]{:S(2)}) copy-start(f32[8,64]{1,0:T(8,128)} %prev_left.1) | copy-start | bytes 6148
  0.7 22.9 %copy-start.1 = (f32[8,64]{1,0:T(8,128)S(1)}, f32[8,64]{1,0:T(8,128)}, u32[]{:S(2)}) copy-start(f32[8,64]{1,0:T(8,128)} %prev_right.1) | copy-start | bytes 6148
  24.0 5.4 %collective-permute-start = (bf16[16,1536]{1,0:T(8,128)(2,1)S(1)}, bf16[16,1536]{1,0:T(8,128)(2,1)S(1)}, u32[]{:S(2)}, u32[]{:S(2)}) collective-permute-start(bf16[16,1536]{1,0:T(8,128)(2,1)S(1)} %get-tuple-element.29), channel_id=1, source_target_pairs={{0,0},{1,16},{2,32},{3,48},{4,64},{5,80},{6,96},{7,112},{8,128},{9... | collective-permute-start | bytes 147464 | tf_op jit(solution)/shard_map/ppermute | solution.py:229

commit v4 on v3

--- a/solution.py
+++ b/solution.py
@@ -7,7 +7,9 @@
 from jax.experimental.pallas import tpu as pltpu
 from jax.sharding import PartitionSpec as P
 
-AXES = ("row", "col")
+ROW = ("row",)
+COL = ("chip", "core")
+AXES = ROW + COL
 HALF = 64
 LANES = 128
 CANCEL = 1e-3
@@ -199,8 +201,8 @@
 
 
 def local(amplitudes_right, amplitudes_left, previous_right, previous_left, coupling, ladder):
-    count = lax.axis_size("col")
-    devices = lax.axis_size("row") * count
+    count = lax.axis_size(COL)
+    devices = lax.axis_size(ROW) * count
     pairs_total = amplitudes_right.shape[1] * devices
     wide = jax.ShapeDtypeStruct((count, 8, LANES), jnp.float32)
     thin = jax.ShapeDtypeStruct((count, 8, LANES), jnp.bfloat16)
@@ -218,7 +220,7 @@
             cost_estimate=pl.CostEstimate(flops=10_000_000_000, bytes_accessed=65_536, transcendentals=0),
             compiler_params=PARAMS,
         )(stay(amplitudes_right), stay(amplitudes_left))
-    gathered = lax.all_to_all(chunks, "col", 0, 0, tiled=True)
+    gathered = lax.all_to_all(chunks, COL, 0, 0, tiled=True)
     with jax.named_scope("left_product"):
         packed, damped = pl.pallas_call(
             left_kernel, out_shape=(folded, tile), in_specs=[VMEM] * 5,
@@ -232,14 +234,17 @@
             right_kernel, out_shape=wide, in_specs=[VMEM] * 2, out_specs=VMEM,
             compiler_params=PARAMS,
         )(turned, ladder)
-    partials = lax.all_to_all(partials, "col", 0, 0, tiled=True)
+    partials = lax.all_to_all(partials, COL, 0, 0, tiled=True)
     with jax.named_scope("inner_products"):
         rows, reduced = pl.pallas_call(
             products_kernel,
-            out_shape=(jax.ShapeDtypeStruct((devices, LANES), jnp.float32), tile),
+            out_shape=(tile, tile),
             in_specs=[VMEM] * 3, out_specs=(VMEM,) * 2, compiler_params=PARAMS,
         )(partials, both, damped)
-    rows = lax.all_to_all(rows, AXES, 0, 0, tiled=True)
+    other = lax.ppermute(rows, "core", ((0, 1), (1, 0)))
+    with jax.named_scope("chip_total"):
+        rows = jnp.broadcast_to((rows + other)[:1], (devices // 2, LANES))
+    rows = lax.all_to_all(rows, ROW + COL[:1], 0, 0, tiled=True)
     half_out = pltpu.HBM((8, HALF), jnp.float32)
     with jax.named_scope("finish"):
         next_right, next_left, coefficients, flag = pl.pallas_call(
@@ -263,13 +268,15 @@
 
 
 def solution(mesh):
+    rows_count, cols_count = mesh.devices.shape
+    mesh = jax.sharding.Mesh(mesh.devices.reshape(rows_count, cols_count // 2, 2), ROW + COL)
     placed = (
         P(None, AXES),
         P(None, AXES),
         P(None, AXES),
         P(None, AXES),
         P(),
-        P("row", "col"),
+        P(ROW, COL),
     )
     return jax.shard_map(
         local,

time: 71.1 us -> 70.7 us (level)
  blocking collectives: 61.6 us -> 59.8 us
  waiting for transfers between devices: 1.92 us -> 2.74 us
    all_to_all x3, blocking collectives: 61.6 us -> 59.8 us  [the longest x1 21.9 us: local(): gathered = lax.all_to_all(chunks, COL, 0, 0, tiled=True)]
    ppermute x0 -> x1, waiting for transfers between devices: none -> 0.82 us  [local(): other = lax.ppermute(rows, 'core', ((0, 1), (1, 0)))]
  transfers between devices with their start and end apart: 1 -> 2, of which waited for: 1 -> 2; matrix products, arithmetic and copies ran while one was open for 0% -> 0% of each run, Pallas kernels for 0% -> 0%
where the time goes in v4:
time: 70.7 us; the launch traced here: 70.4 us
  blocking collectives  59.8 us (85%)
  starting transfers between devices  4 us (6%)
  Pallas kernels  3.12 us (4%)
  waiting for transfers between devices  2.74 us (4%)
  between operations  0.73 us (1%)
    all_to_all x1, blocking collectives, local(): gathered = lax.all_to_all(chunks, COL, 0, 0, tiled=True)  21.9 us
    all_to_all x1, blocking collectives, local(): partials = lax.all_to_all(partials, COL, 0, 0, tiled=True)  20.3 us
    all_to_all x1, blocking collectives, local(): rows = lax.all_to_all(rows, ROW + COL[:1], 0, 0, tiled=True)  17.5 us
    ppermute x1, starting transfers between devices, local(): turned = lax.ppermute(packed, AXES, transpose)  3.48 us
    ppermute x1, waiting for transfers between devices, local(): turned = lax.ppermute(packed, AXES, transpose)  1.92 us
  transfers between devices with their start and end apart: 2, of which 2 were waited for; matrix products, arithmetic and copies ran while one was open for 0% of the time, Pallas kernels for 0%

profile of v4, /device:TPU:1, one launch (start us, length us, event | category | flops | bytes accessed | tf_op | source)
XLA Modules:
  0.0 70.4 jit_solution(11531760423597977152)
XLA Ops:
  0.6 0.0 copy-start
  0.6 0.0 copy-start.3
  0.7 0.0 copy-start.2
  0.7 0.0 copy-start.1
  0.7 0.9 %pack.1 = (bf16[16,8,128]{2,1,0:T(8,128)(2,1)S(1)}, f32[8,128]{1,0:T(8,128)S(1)}) custom-call(f32[8,64]{1,0:T(8,128)} %right.1, f32[8,64]{1,0:T(8,128)} %left.1), custom_call_target="tpu_custom_call" | custom-call | flops 10000000000 | bytes 65536 | tf_op jit(solution)/shard_map/pack/pallas_call | solution.py:217
  1.6 21.9 %all_to_all.18.gathered = bf16[16,8,128]{2,1,0:T(8,128)(2,1)S(1)} all-to-all(bf16[16,8,128]{2,1,0:T(8,128)(2,1)S(1)} %get-tuple-element.28), channel_id=1, replica_groups=mesh['row'=16,'chip'=8,'core'=2] {'chip','core'}, dimensions={0} | all-to-all | bytes 65536 | tf_op jit(solution)/shard_map/all_to_all | solution.py:223
  23.6 0.0 copy-done
  23.6 0.0 copy-done.3
  23.6 0.0 copy-done.2
  23.6 0.0 copy-done.1
  23.6 0.4 left_product.1
  24.0 3.5 %collective-permute-start = (bf16[16,1536]{1,0:T(8,128)(2,1)S(1)}, bf16[16,1536]{1,0:T(8,128)(2,1)S(1)}, u32[]{:S(2)}, u32[]{:S(2)}) collective-permute-start(bf16[16,1536]{1,0:T(8,128)(2,1)S(1)} %get-tuple-element.29), channel_id=1, source_target_pairs={{0,0},{1,16},{2,32},{3,48},{4,64},{5,80},{6,96},{7,112},{8,128},{9... | collective-permute-start | bytes 147464 | tf_op jit(solution)/shard_map/ppermute | solution.py:231
  27.5 1.9 %collective-permute-done.turned = bf16[16,1536]{1,0:T(8,128)(2,1)S(1)} collective-permute-done((bf16[16,1536]{1,0:T(8,128)(2,1)S(1)}, bf16[16,1536]{1,0:T(8,128)(2,1)S(1)}, u32[]{:S(2)}, u32[]{:S(2)}) %collective-permute-start) | collective-permute-done | bytes 49184 | tf_op jit(solution)/shard_map/ppermute | solution.py:231
  29.4 0.7 %right_product.1 = f32[16,8,128]{2,1,0:T(8,128)S(1)} custom-call(bf16[16,1536]{1,0:T(8,128)(2,1)S(1)} %collective-permute-done.turned, bf16[1024,1024]{1,0:T(8,128)(2,1)S(1)} %copy-done), custom_call_target="tpu_custom_call" | custom-call | tf_op jit(solution)/shard_map/right_product/pallas_call | solution.py:233
  30.1 20.3 %all_to_all.19.partials = f32[16,8,128]{2,1,0:T(8,128)S(1)} all-to-all(f32[16,8,128]{2,1,0:T(8,128)S(1)} %right_product.1), channel_id=1, replica_groups=mesh['row'=16,'chip'=8,'core'=2] {'chip','core'}, dimensions={0} | all-to-all | bytes 131072 | tf_op jit(solution)/shard_map/all_to_all | solution.py:237
  50.4 0.2 inner_products.1
  50.6 0.5 collective-permute-start.1
  51.1 0.8 %collective-permute-done.1 = f32[8,128]{1,0:T(8,128)S(1)} collective-permute-done((f32[8,128]{1,0:T(8,128)S(1)}, f32[8,128]{1,0:T(8,128)S(1)}, u32[]{:S(2)}, u32[]{:S(2)}) %collective-permute-start.1) | collective-permute-done | bytes 4128 | tf_op jit(solution)/shard_map/ppermute | solution.py:244
  52.0 17.5 %all_to_all.20 = f32[128,1,128]{2,1,0:T(1,128)S(1)} all-to-all(f32[128,1,128]{2,1,0:T(1,128)S(1)} %broadcast_in_dim.2), channel_id=1, replica_groups=mesh['row'=16,'chip'=8,'core'=2] {'row','chip'}, dimensions={0} | all-to-all | bytes 131072 | tf_op jit(solution)/shard_map/all_to_all | solution.py:247
  69.5 0.9 %finish.1 = (f32[8,64]{1,0:T(8,128)}, f32[8,64]{1,0:T(8,128)}, f32[3,8]{1,0:T(4,128)}, s32[1,1]{1,0:T(1,128)S(4)}) custom-call(f32[128,128]{1,0:T(8,128)S(1)} %bitcast.24, f32[8,128]{1,0:T(8,128)S(1)} %get-tuple-element.33.reduced, f32[8,128]{1,0:T(8,128)S(1)} %get-tuple-element.30.both), custom_call_target="tpu_custom_call" | custom-call | tf_op jit(solution)/shard_map/finish/pallas_call | solution.py:250
  (4 shorter events, 0.1 us)
Async XLA Ops:
  0.6 22.9 %copy-start = (bf16[1024,1024]{1,0:T(8,128)(2,1)S(1)}, bf16[1024,1024]{1,0:T(8,128)(2,1)}, u32[]{:S(2)}) copy-start(bf16[1024,1024]{1,0:T(8,128)(2,1)} %ladder.3) | copy-start | bytes 6291460
  0.6 22.9 %copy-start.3 = (f32[2,8]{1,0:T(2,128)S(1)}, f32[2,8]{1,0:T(2,128)}, u32[]{:S(2)}) copy-start(f32[2,8]{1,0:T(2,128)} %coupling.1) | copy-start | bytes 196
  0.7 22.9 %copy-start.2 = (f32[8,64]{1,0:T(8,128)S(1)}, f32[8,64]{1,0:T(8,128)}, u32[]{:S(2)}) copy-start(f32[8,64]{1,0:T(8,128)} %prev_left.1) | copy-start | bytes 6148
  0.7 22.9 %copy-start.1 = (f32[8,64]{1,0:T(8,128)S(1)}, f32[8,64]{1,0:T(8,128)}, u32[]{:S(2)}) copy-start(f32[8,64]{1,0:T(8,128)} %prev_right.1) | copy-start | bytes 6148
  24.0 5.4 %collective-permute-start = (bf16[16,1536]{1,0:T(8,128)(2,1)S(1)}, bf16[16,1536]{1,0:T(8,128)(2,1)S(1)}, u32[]{:S(2)}, u32[]{:S(2)}) collective-permute-start(bf16[16,1536]{1,0:T(8,128)(2,1)S(1)} %get-tuple-element.29), channel_id=1, source_target_pairs={{0,0},{1,16},{2,32},{3,48},{4,64},{5,80},{6,96},{7,112},{8,128},{9... | collective-permute-start | bytes 147464 | tf_op jit(solution)/shard_map/ppermute | solution.py:231
  50.6 1.3 %collective-permute-start.1 = (f32[8,128]{1,0:T(8,128)S(1)}, f32[8,128]{1,0:T(8,128)S(1)}, u32[]{:S(2)}, u32[]{:S(2)}) collective-permute-start(f32[8,128]{1,0:T(8,128)S(1)} %get-tuple-element.32), channel_id=1, source_target_pairs={{0,1},{1,0},{2,3},{3,2},{4,5},{5,4},{6,7},{7,6},{8,9},{9,8},{10,11... | collective-permute-start | bytes 12296 | tf_op jit(solution)/shard_map/ppermute | solution.py:244

commit v5 on v4

--- a/solution.py
+++ b/solution.py
@@ -8,7 +8,7 @@
 from jax.sharding import PartitionSpec as P
 
 ROW = ("row",)
-COL = ("chip", "core")
+COL = ("far", "chip", "core")
 AXES = ROW + COL
 HALF = 64
 LANES = 128
@@ -45,19 +45,31 @@
     return copies
 
 
-def pack_kernel(right, left, chunks, both, right_here, left_here, sems):
-    for copy in fetch((right, left), (right_here, left_here), sems):
+def pack_kernel(
+    right, left, prev_right, prev_left, coupling,
+    chunks, both, right_here, left_here, prev_right_here, prev_left_here, coupling_here, sems,
+):
+    sources = (right, left, prev_right, prev_left, coupling)
+    targets = (right_here, left_here, prev_right_here, prev_left_here, coupling_here)
+    for copy in fetch(sources, targets, sems):
         copy.wait()
     tile = jnp.concatenate([right_here[...], left_here[...]], axis=1)
+    damped = jnp.concatenate(
+        [
+            column_of(coupling_here[1:2, :]) * prev_right_here[...],
+            column_of(coupling_here[0:1, :]) * prev_left_here[...],
+        ],
+        axis=1,
+    )
     both[...] = tile
-    chunks[...] = jnp.broadcast_to(tile.astype(jnp.bfloat16)[None], chunks.shape)
-
-
-def left_kernel(gathered, ladder, prev_right, prev_left, coupling, out, damped):
+    chunks[...] = jnp.broadcast_to(jnp.concatenate([tile, damped], axis=0)[None], chunks.shape)
+
+
+def left_kernel(gathered, ladder, out):
     low = lane_of((8, LANES)) < HALF
     rights, lefts = [], []
     for m in range(gathered.shape[0] // 2):
-        even, odd = gathered[2 * m].astype(jnp.float32), gathered[2 * m + 1].astype(jnp.float32)
+        even, odd = gathered[2 * m, :8], gathered[2 * m + 1, :8]
         rights.append(jnp.where(low, even, swap(odd)))
         lefts.append(jnp.where(low, swap(even), odd))
     block = jnp.concatenate(lefts, axis=1).astype(jnp.bfloat16)
@@ -68,13 +80,6 @@
     upper = jnp.concatenate(rights + [rest[:, : width // 2]], axis=1)
     lower = jnp.concatenate([high, rest[:, width // 2 :]], axis=1)
     out[...] = jnp.concatenate([upper, lower], axis=0).astype(jnp.bfloat16)
-    damped[...] = jnp.concatenate(
-        [
-            column_of(coupling[1:2, :]) * prev_right[...],
-            column_of(coupling[0:1, :]) * prev_left[...],
-        ],
-        axis=1,
-    )
 
 
 def right_kernel(turned, ladder, out):
@@ -84,6 +89,7 @@
     terms = lax.dot_general(
         block, ladder[...], (((1,), (1,)), ((), ())), preferred_element_type=jnp.float32
     )
+    tiles = []
     for m in range(out.shape[0] // 2):
         at = LANES * m
         side = at % (width // 2)
@@ -92,19 +98,39 @@
         rest = turned[:, width + side : width + side + LANES].astype(jnp.float32)[half : half + 8]
         left = high + rest
         piece = terms[:, at : at + LANES]
-        out[2 * m] = jnp.where(low, piece, swap(left))
-        out[2 * m + 1] = jnp.where(low, swap(piece), left)
-
-
-def products_kernel(partials, both, damped, rows, reduced):
+        tiles.append(jnp.where(low, piece, swap(left)))
+        tiles.append(jnp.where(low, swap(piece), left))
+    half = len(tiles) // 2
+    for at, tile in enumerate(tiles):
+        for far in range(2):
+            out[far * half + at % half, at // half] = tile
+
+
+def products_kernel(partials, gathered, rows, reduced):
     shape = (8, LANES)
     lane = lane_of(shape)
     low = lane < HALF
-    image = jnp.sum(partials[...], axis=0)
-    pair = both[...]
-    crossed = swap(pair)
-    work = image - damped[...]
-    reduced[...] = work
+    half = partials.shape[0] // 2
+    near = lax.axis_index("chip") * lax.axis_size("core") + lax.axis_index("core")
+    mine = lax.axis_index("far")
+    tiles = [0.0] * 7
+    for far in range(2):
+        chunk = gathered[far * half + near]
+        pair, damped = chunk[:8], chunk[8:]
+        image = jnp.sum(partials[:, far], axis=0)
+        crossed = swap(pair)
+        work = image - damped
+
+        @pl.when(mine == far)
+        def _(work=work):
+            reduced[...] = work
+
+        terms = (
+            image * crossed, work * swap(work), work * crossed, pair * crossed,
+            work * work, work * pair, pair * pair,
+        )
+        tiles = [tile + term for tile, term in zip(tiles, terms, strict=True)]
+    first, cross, mixed, base_cross, square, own, base = tiles
 
     def total(tile):
         return jnp.sum(tile, axis=1, keepdims=True)
@@ -115,20 +141,9 @@
     def upper(tile):
         return total(jnp.where(low, 0.0, tile))
 
-    own = work * pair
-    square = work * work
-    base = pair * pair
     dots = (
-        lower(image * crossed),
-        lower(work * swap(work)),
-        total(work * crossed),
-        lower(pair * crossed),
-        lower(square),
-        lower(own),
-        lower(base),
-        upper(square),
-        upper(own),
-        upper(base),
+        lower(first), lower(cross), total(mixed), lower(base_cross), lower(square),
+        lower(own), lower(base), upper(square), upper(own), upper(base),
     )
     slot = lane // 8
     table = jnp.zeros(shape, jnp.float32)
@@ -204,8 +219,6 @@
     count = lax.axis_size(COL)
     devices = lax.axis_size(ROW) * count
     pairs_total = amplitudes_right.shape[1] * devices
-    wide = jax.ShapeDtypeStruct((count, 8, LANES), jnp.float32)
-    thin = jax.ShapeDtypeStruct((count, 8, LANES), jnp.bfloat16)
     block = ladder.shape[1]
     folded = jax.ShapeDtypeStruct((16, block + block // 2), jnp.bfloat16)
     tile = jax.ShapeDtypeStruct((8, LANES), jnp.float32)
@@ -215,23 +228,30 @@
     stay = functools.partial(pltpu.with_memory_space_constraint, memory_space=pltpu.HBM)
     with jax.named_scope("pack"):
         chunks, both = pl.pallas_call(
-            pack_kernel, out_shape=(thin, tile), in_specs=[HBM] * 2, out_specs=(VMEM,) * 2,
-            scratch_shapes=[half, half, pltpu.SemaphoreType.DMA((2,))],
-            cost_estimate=pl.CostEstimate(flops=10_000_000_000, bytes_accessed=65_536, transcendentals=0),
+            pack_kernel,
+            out_shape=(jax.ShapeDtypeStruct((count, 16, LANES), jnp.float32), tile),
+            in_specs=[HBM] * 5, out_specs=(VMEM,) * 2,
+            scratch_shapes=[half] * 4
+            + [pltpu.VMEM((2, 8), jnp.float32), pltpu.SemaphoreType.DMA((5,))],
+            cost_estimate=pl.CostEstimate(
+                flops=10_000_000_000, bytes_accessed=65_536, transcendentals=0
+            ),
             compiler_params=PARAMS,
-        )(stay(amplitudes_right), stay(amplitudes_left))
+        )(
+            stay(amplitudes_right), stay(amplitudes_left), stay(previous_right),
+            stay(previous_left), stay(coupling),
+        )
     gathered = lax.all_to_all(chunks, COL, 0, 0, tiled=True)
     with jax.named_scope("left_product"):
-        packed, damped = pl.pallas_call(
-            left_kernel, out_shape=(folded, tile), in_specs=[VMEM] * 5,
-            out_specs=(VMEM,) * 2,
+        packed = pl.pallas_call(
+            left_kernel, out_shape=folded, in_specs=[VMEM] * 2, out_specs=VMEM,
             compiler_params=PARAMS,
-        )(gathered, ladder, previous_right, previous_left, coupling)
+        )(gathered, ladder)
     transpose = [(i * count + j, j * count + i) for i in range(count) for j in range(count)]
     turned = lax.ppermute(packed, AXES, transpose)
     with jax.named_scope("right_product"):
         partials = pl.pallas_call(
-            right_kernel, out_shape=wide, in_specs=[VMEM] * 2, out_specs=VMEM,
+            right_kernel, out_shape=jax.ShapeDtypeStruct((count, 2, 8, LANES), jnp.float32), in_specs=[VMEM] * 2, out_specs=VMEM,
             compiler_params=PARAMS,
         )(turned, ladder)
     partials = lax.all_to_all(partials, COL, 0, 0, tiled=True)
@@ -239,12 +259,12 @@
         rows, reduced = pl.pallas_call(
             products_kernel,
             out_shape=(tile, tile),
-            in_specs=[VMEM] * 3, out_specs=(VMEM,) * 2, compiler_params=PARAMS,
-        )(partials, both, damped)
+            in_specs=[VMEM] * 2, out_specs=(VMEM,) * 2, compiler_params=PARAMS,
+        )(partials, gathered)
     other = lax.ppermute(rows, "core", ((0, 1), (1, 0)))
     with jax.named_scope("chip_total"):
-        rows = jnp.broadcast_to((rows + other)[:1], (devices // 2, LANES))
-    rows = lax.all_to_all(rows, ROW + COL[:1], 0, 0, tiled=True)
+        rows = jnp.broadcast_to((rows + other)[:1], (devices // 4, LANES))
+    rows = lax.all_to_all(rows, ROW + COL[1:2], 0, 0, tiled=True)
     half_out = pltpu.HBM((8, HALF), jnp.float32)
     with jax.named_scope("finish"):
         next_right, next_left, coefficients, flag = pl.pallas_call(
@@ -269,7 +289,7 @@
 
 def solution(mesh):
     rows_count, cols_count = mesh.devices.shape
-    mesh = jax.sharding.Mesh(mesh.devices.reshape(rows_count, cols_count // 2, 2), ROW + COL)
+    mesh = jax.sharding.Mesh(mesh.devices.reshape(rows_count, 2, cols_count // 4, 2), ROW + COL)
     placed = (
         P(None, AXES),
         P(None, AXES),

time: 70.7 us -> 70.4 us (level)
  blocking collectives: 59.8 us -> 59 us
    all_to_all x1, blocking collectives: 17.5 us -> 16.1 us  [local(): rows = lax.all_to_all(rows, ROW + COL[1:2], 0, 0, tiled=True)]
where the time goes in v5:
time: 70.4 us; the launch traced here: 70.2 us
  blocking collectives  59 us (84%)
  starting transfers between devices  4.51 us (6%)
  Pallas kernels  3.39 us (5%)
  waiting for transfers between devices  2.58 us (4%)
    all_to_all x1, blocking collectives, local(): gathered = lax.all_to_all(chunks, COL, 0, 0, tiled=True)  22.4 us
    all_to_all x1, blocking collectives, local(): partials = lax.all_to_all(partials, COL, 0, 0, tiled=True)  20.5 us
    all_to_all x1, blocking collectives, local(): rows = lax.all_to_all(rows, ROW + COL[1:2], 0, 0, tiled=True)  16.1 us
    ppermute x1, starting transfers between devices, local(): turned = lax.ppermute(packed, AXES, transpose)  3.74 us
    ppermute x1, waiting for transfers between devices, local(): turned = lax.ppermute(packed, AXES, transpose)  1.76 us
  transfers between devices with their start and end apart: 2, of which 2 were waited for; matrix products, arithmetic and copies ran while one was open for 0% of the time, Pallas kernels for 0%

profile of v5, /device:TPU:1, one launch (start us, length us, event | category | flops | bytes accessed | tf_op | source)
XLA Modules:
  0.0 70.2 jit_solution(9706863525750239704)
XLA Ops:
  0.6 0.0 copy-start
  0.6 1.1 %pack.1 = (f32[16,16,128]{2,1,0:T(8,128)S(1)}, f32[8,128]{1,0:T(8,128)S(1)}) custom-call(f32[8,64]{1,0:T(8,128)} %right.1, f32[8,64]{1,0:T(8,128)} %left.1, f32[8,64]{1,0:T(8,128)} %prev_right.1, f32[8,64]{1,0:T(8,128)} %prev_left.1, f32[2,8]{1,0:T(2,128)} %coupling.1), custom_call_target="tpu_custom_call" | custom-call | flops 10000000000 | bytes 65536 | tf_op jit(solution)/shard_map/pack/pallas_call | solution.py:230
  1.7 22.4 %all_to_all.18.gathered = f32[16,16,128]{2,1,0:T(8,128)S(1)} all-to-all(f32[16,16,128]{2,1,0:T(8,128)S(1)} %get-tuple-element.26), channel_id=1, replica_groups=mesh['row'=16,'far'=2,'chip'=4,'core'=2] {'far','chip','core'}, dimensions={0} | all-to-all | bytes 262144 | tf_op jit(solution)/shard_map/all_to_all | solution.py:244
  24.1 0.0 copy-done
  24.1 0.4 left_product.1
  24.6 3.7 %collective-permute-start = (bf16[16,1536]{1,0:T(8,128)(2,1)S(1)}, bf16[16,1536]{1,0:T(8,128)(2,1)S(1)}, u32[]{:S(2)}, u32[]{:S(2)}) collective-permute-start(bf16[16,1536]{1,0:T(8,128)(2,1)S(1)} %left_product.1), channel_id=1, source_target_pairs={{0,0},{1,16},{2,32},{3,48},{4,64},{5,80},{6,96},{7,112},{8,128},{9... | collective-permute-start | bytes 147464 | tf_op jit(solution)/shard_map/ppermute | solution.py:251
  28.3 1.8 %collective-permute-done.turned = bf16[16,1536]{1,0:T(8,128)(2,1)S(1)} collective-permute-done((bf16[16,1536]{1,0:T(8,128)(2,1)S(1)}, bf16[16,1536]{1,0:T(8,128)(2,1)S(1)}, u32[]{:S(2)}, u32[]{:S(2)}) %collective-permute-start) | collective-permute-done | bytes 49184 | tf_op jit(solution)/shard_map/ppermute | solution.py:251
  30.1 0.7 %right_product.1 = f32[16,2,8,128]{3,2,1,0:T(8,128)S(1)} custom-call(bf16[16,1536]{1,0:T(8,128)(2,1)S(1)} %collective-permute-done.turned, bf16[1024,1024]{1,0:T(8,128)(2,1)S(1)} %copy-done), custom_call_target="tpu_custom_call" | custom-call | tf_op jit(solution)/shard_map/right_product/pallas_call | solution.py:253
  30.8 20.5 %all_to_all.19.partials = f32[16,2,8,128]{3,2,1,0:T(8,128)S(1)} all-to-all(f32[16,2,8,128]{3,2,1,0:T(8,128)S(1)} %right_product.1), channel_id=1, replica_groups=mesh['row'=16,'far'=2,'chip'=4,'core'=2] {'far','chip','core'}, dimensions={0} | all-to-all | bytes 262144 | tf_op jit(solution)/shard_map/all_to_all | solution.py:257
  51.3 0.3 inner_products.1
  51.6 0.8 %collective-permute-start.1 = (f32[8,128]{1,0:T(8,128)S(1)}, f32[8,128]{1,0:T(8,128)S(1)}, u32[]{:S(2)}, u32[]{:S(2)}) collective-permute-start(f32[8,128]{1,0:T(8,128)S(1)} %get-tuple-element.27), channel_id=1, source_target_pairs={{0,1},{1,0},{2,3},{3,2},{4,5},{5,4},{6,7},{7,6},{8,9},{9,8},{10,11... | collective-permute-start | bytes 12296 | tf_op jit(solution)/shard_map/ppermute | solution.py:264
  52.4 0.8 %collective-permute-done.1 = f32[8,128]{1,0:T(8,128)S(1)} collective-permute-done((f32[8,128]{1,0:T(8,128)S(1)}, f32[8,128]{1,0:T(8,128)S(1)}, u32[]{:S(2)}, u32[]{:S(2)}) %collective-permute-start.1) | collective-permute-done | bytes 4128 | tf_op jit(solution)/shard_map/ppermute | solution.py:264
  53.2 16.1 %all_to_all.20 = f32[64,1,128]{2,1,0:T(1,128)S(1)} all-to-all(f32[64,1,128]{2,1,0:T(1,128)S(1)} %broadcast_in_dim.2), channel_id=1, replica_groups=mesh['row'=16,'far'=2,'chip'=4,'core'=2] {'row','chip'}, dimensions={0} | all-to-all | bytes 65536 | tf_op jit(solution)/shard_map/all_to_all | solution.py:267
  69.3 0.9 %finish.1 = (f32[8,64]{1,0:T(8,128)}, f32[8,64]{1,0:T(8,128)}, f32[3,8]{1,0:T(4,128)}, s32[1,1]{1,0:T(1,128)S(4)}) custom-call(f32[64,128]{1,0:T(8,128)S(1)} %bitcast.24, f32[8,128]{1,0:T(8,128)S(1)} %get-tuple-element.28.reduced, f32[8,128]{1,0:T(8,128)S(1)} %get-tuple-element.29.both), custom_call_target="tpu_custom_call" | custom-call | tf_op jit(solution)/shard_map/finish/pallas_call | solution.py:270
  (4 shorter events, 0.0 us)
Async XLA Ops:
  0.6 23.5 %copy-start = (bf16[1024,1024]{1,0:T(8,128)(2,1)S(1)}, bf16[1024,1024]{1,0:T(8,128)(2,1)}, u32[]{:S(2)}) copy-start(bf16[1024,1024]{1,0:T(8,128)(2,1)} %ladder.3) | copy-start | bytes 6291460
  24.6 5.5 %collective-permute-start = (bf16[16,1536]{1,0:T(8,128)(2,1)S(1)}, bf16[16,1536]{1,0:T(8,128)(2,1)S(1)}, u32[]{:S(2)}, u32[]{:S(2)}) collective-permute-start(bf16[16,1536]{1,0:T(8,128)(2,1)S(1)} %left_product.1), channel_id=1, source_target_pairs={{0,0},{1,16},{2,32},{3,48},{4,64},{5,80},{6,96},{7,112},{8,128},{9... | collective-permute-start | bytes 147464 | tf_op jit(solution)/shard_map/ppermute | solution.py:251
  51.6 1.6 %collective-permute-start.1 = (f32[8,128]{1,0:T(8,128)S(1)}, f32[8,128]{1,0:T(8,128)S(1)}, u32[]{:S(2)}, u32[]{:S(2)}) collective-permute-start(f32[8,128]{1,0:T(8,128)S(1)} %get-tuple-element.27), channel_id=1, source_target_pairs={{0,1},{1,0},{2,3},{3,2},{4,5},{5,4},{6,7},{7,6},{8,9},{9,8},{10,11... | collective-permute-start | bytes 12296 | tf_op jit(solution)/shard_map/ppermute | solution.py:264

commit v6 on v5

--- a/solution.py
+++ b/solution.py
@@ -12,6 +12,7 @@
 AXES = ROW + COL
 HALF = 64
 LANES = 128
+CHUNK = 17
 CANCEL = 1e-3
 VMEM = pl.BlockSpec(memory_space=pltpu.VMEM)
 HBM = pl.BlockSpec(memory_space=pltpu.HBM)
@@ -45,31 +46,21 @@
     return copies
 
 
-def pack_kernel(
-    right, left, prev_right, prev_left, coupling,
-    chunks, both, right_here, left_here, prev_right_here, prev_left_here, coupling_here, sems,
-):
-    sources = (right, left, prev_right, prev_left, coupling)
-    targets = (right_here, left_here, prev_right_here, prev_left_here, coupling_here)
-    for copy in fetch(sources, targets, sems):
+def pack_kernel(right, left, chunks, both, right_here, left_here, sems):
+    for copy in fetch((right, left), (right_here, left_here), sems):
         copy.wait()
     tile = jnp.concatenate([right_here[...], left_here[...]], axis=1)
-    damped = jnp.concatenate(
-        [
-            column_of(coupling_here[1:2, :]) * prev_right_here[...],
-            column_of(coupling_here[0:1, :]) * prev_left_here[...],
-        ],
-        axis=1,
-    )
     both[...] = tile
-    chunks[...] = jnp.broadcast_to(jnp.concatenate([tile, damped], axis=0)[None], chunks.shape)
-
-
-def left_kernel(gathered, ladder, out):
+    chunks[...] = jnp.broadcast_to(tile[None], chunks.shape)
+
+
+def left_kernel(
+    gathered, ladder, both, prev_right, prev_left, coupling, out, damped, missing
+):
     low = lane_of((8, LANES)) < HALF
     rights, lefts = [], []
     for m in range(gathered.shape[0] // 2):
-        even, odd = gathered[2 * m, :8], gathered[2 * m + 1, :8]
+        even, odd = gathered[2 * m], gathered[2 * m + 1]
         rights.append(jnp.where(low, even, swap(odd)))
         lefts.append(jnp.where(low, swap(even), odd))
     block = jnp.concatenate(lefts, axis=1).astype(jnp.bfloat16)
@@ -80,9 +71,21 @@
     upper = jnp.concatenate(rights + [rest[:, : width // 2]], axis=1)
     lower = jnp.concatenate([high, rest[:, width // 2 :]], axis=1)
     out[...] = jnp.concatenate([upper, lower], axis=0).astype(jnp.bfloat16)
-
-
-def right_kernel(turned, ladder, out):
+    tile = jnp.concatenate(
+        [
+            column_of(coupling[1:2, :]) * prev_right[...],
+            column_of(coupling[0:1, :]) * prev_left[...],
+        ],
+        axis=1,
+    )
+    damped[...] = tile
+    lane = lane_of((8, LANES))
+    lack = jnp.sum(jnp.where(low, tile * swap(both[...]), 0.0), axis=1, keepdims=True)
+    spread = jnp.where(lane == sublane_of((8, LANES)), lack, 0.0)
+    missing[...] = jnp.sum(spread, axis=0, keepdims=True)
+
+
+def right_kernel(turned, ladder, damped, missing, out):
     low = lane_of((8, LANES)) < HALF
     width = ladder.shape[1]
     block = turned[:, :width][:8]
@@ -90,7 +93,7 @@
         block, ladder[...], (((1,), (1,)), ((), ())), preferred_element_type=jnp.float32
     )
     tiles = []
-    for m in range(out.shape[0] // 2):
+    for m in range(width // LANES):
         at = LANES * m
         side = at % (width // 2)
         half = 8 * (at // (width // 2))
@@ -101,36 +104,47 @@
         tiles.append(jnp.where(low, piece, swap(left)))
         tiles.append(jnp.where(low, swap(piece), left))
     half = len(tiles) // 2
+    near = lax.axis_index("chip") * lax.axis_size("core") + lax.axis_index("core")
+    mine = lax.axis_index("far") * half + near
+    own = damped[...]
     for at, tile in enumerate(tiles):
+        tile = tile - jnp.where(mine == at, own, 0.0)
         for far in range(2):
-            out[far * half + at % half, at // half] = tile
+            start = CHUNK * (far * half + at % half) + 8 * (at // half)
+            out[start : start + 8, :] = tile
+    for at in range(len(tiles)):
+        out[CHUNK * at + 16 : CHUNK * at + 17, :] = missing[...]
 
 
 def products_kernel(partials, gathered, rows, reduced):
     shape = (8, LANES)
     lane = lane_of(shape)
     low = lane < HALF
-    half = partials.shape[0] // 2
+    count = gathered.shape[0]
+    half = count // 2
     near = lax.axis_index("chip") * lax.axis_size("core") + lax.axis_index("core")
     mine = lax.axis_index("far")
-    tiles = [0.0] * 7
+    tiles = [0.0] * 6
     for far in range(2):
-        chunk = gathered[far * half + near]
-        pair, damped = chunk[:8], chunk[8:]
-        image = jnp.sum(partials[:, far], axis=0)
+        pair = gathered[far * half + near]
         crossed = swap(pair)
-        work = image - damped
+        work = partials[8 * far : 8 * far + 8, :]
+        for at in range(1, count):
+            work = work + partials[CHUNK * at + 8 * far : CHUNK * at + 8 * far + 8, :]
 
         @pl.when(mine == far)
         def _(work=work):
             reduced[...] = work
 
         terms = (
-            image * crossed, work * swap(work), work * crossed, pair * crossed,
-            work * work, work * pair, pair * pair,
+            work * swap(work), work * crossed, pair * crossed, work * work,
+            work * pair, pair * pair,
         )
         tiles = [tile + term for tile, term in zip(tiles, terms, strict=True)]
-    first, cross, mixed, base_cross, square, own, base = tiles
+    cross, mixed, base_cross, square, own, base = tiles
+    lack = partials[16:17, :]
+    for at in range(1, count):
+        lack = lack + partials[CHUNK * at + 16 : CHUNK * at + 17, :]
 
     def total(tile):
         return jnp.sum(tile, axis=1, keepdims=True)
@@ -142,7 +156,7 @@
         return total(jnp.where(low, 0.0, tile))
 
     dots = (
-        lower(first), lower(cross), total(mixed), lower(base_cross), lower(square),
+        lower(mixed), lower(cross), total(mixed), lower(base_cross), lower(square),
         lower(own), lower(base), upper(square), upper(own), upper(base),
     )
     slot = lane // 8
@@ -150,6 +164,7 @@
     for at, dot in enumerate(dots):
         table = jnp.where(slot == at, dot, table)
     row = jnp.sum(jnp.where(lane % 8 == sublane_of(shape), table, 0.0), axis=0, keepdims=True)
+    row = row + jnp.where(lane[:1] < 8, lack * (1.0 / half), 0.0)
     rows[...] = jnp.broadcast_to(row, rows.shape)
 
 
@@ -226,35 +241,32 @@
 
     half = pltpu.VMEM((8, HALF), jnp.float32)
     stay = functools.partial(pltpu.with_memory_space_constraint, memory_space=pltpu.HBM)
+    wide = jax.ShapeDtypeStruct((count, 8, LANES), jnp.float32)
     with jax.named_scope("pack"):
         chunks, both = pl.pallas_call(
-            pack_kernel,
-            out_shape=(jax.ShapeDtypeStruct((count, 16, LANES), jnp.float32), tile),
-            in_specs=[HBM] * 5, out_specs=(VMEM,) * 2,
-            scratch_shapes=[half] * 4
-            + [pltpu.VMEM((2, 8), jnp.float32), pltpu.SemaphoreType.DMA((5,))],
+            pack_kernel, out_shape=(wide, tile), in_specs=[HBM] * 2, out_specs=(VMEM,) * 2,
+            scratch_shapes=[half, half, pltpu.SemaphoreType.DMA((2,))],
             cost_estimate=pl.CostEstimate(
                 flops=10_000_000_000, bytes_accessed=65_536, transcendentals=0
             ),
             compiler_params=PARAMS,
-        )(
-            stay(amplitudes_right), stay(amplitudes_left), stay(previous_right),
-            stay(previous_left), stay(coupling),
-        )
+        )(stay(amplitudes_right), stay(amplitudes_left))
     gathered = lax.all_to_all(chunks, COL, 0, 0, tiled=True)
     with jax.named_scope("left_product"):
-        packed = pl.pallas_call(
-            left_kernel, out_shape=folded, in_specs=[VMEM] * 2, out_specs=VMEM,
-            compiler_params=PARAMS,
-        )(gathered, ladder)
+        packed, damped, missing = pl.pallas_call(
+            left_kernel,
+            out_shape=(folded, tile, jax.ShapeDtypeStruct((1, LANES), jnp.float32)),
+            in_specs=[VMEM] * 6, out_specs=(VMEM,) * 3, compiler_params=PARAMS,
+        )(gathered, ladder, both, previous_right, previous_left, coupling)
     transpose = [(i * count + j, j * count + i) for i in range(count) for j in range(count)]
     turned = lax.ppermute(packed, AXES, transpose)
     with jax.named_scope("right_product"):
         partials = pl.pallas_call(
-            right_kernel, out_shape=jax.ShapeDtypeStruct((count, 2, 8, LANES), jnp.float32), in_specs=[VMEM] * 2, out_specs=VMEM,
-            compiler_params=PARAMS,
-        )(turned, ladder)
-    partials = lax.all_to_all(partials, COL, 0, 0, tiled=True)
+            right_kernel, out_shape=jax.ShapeDtypeStruct((count * CHUNK, LANES), jnp.float32),
+            in_specs=[VMEM] * 4, out_specs=VMEM, compiler_params=PARAMS,
+        )(turned, ladder, damped, missing)
+    partials = partials.reshape(count, CHUNK, 1, LANES)
+    partials = lax.all_to_all(partials, COL, 0, 0, tiled=True).reshape(count * CHUNK, LANES)
     with jax.named_scope("inner_products"):
         rows, reduced = pl.pallas_call(
             products_kernel,

time: 70.4 us -> 70.1 us (level)
  no operation moved by 1% of the time
where the time goes in v6:
time: 70.1 us; the launch traced here: 69.8 us
  blocking collectives  58.8 us (84%)
  starting transfers between devices  4.28 us (6%)
  Pallas kernels  3.26 us (5%)
  waiting for transfers between devices  2.7 us (4%)
  between operations  0.72 us (1%)
    all_to_all x1, blocking collectives, local(): gathered = lax.all_to_all(chunks, COL, 0, 0, tiled=True)  22 us
    all_to_all x1, blocking collectives, local(): lax.all_to_all(partials, COL, 0, 0, tiled=True)  20.8 us
    all_to_all x1, blocking collectives, local(): rows = lax.all_to_all(rows, ROW + COL[1:2], 0, 0, tiled=True)  16 us
    ppermute x1, starting transfers between devices, local(): turned = lax.ppermute(packed, AXES, transpose)  3.52 us
    ppermute x1, waiting for transfers between devices, local(): turned = lax.ppermute(packed, AXES, transpose)  1.87 us
  transfers between devices with their start and end apart: 2, of which 2 were waited for; matrix products, arithmetic and copies ran while one was open for 0% of the time, Pallas kernels for 0%

profile of v6, /device:TPU:1, one launch (start us, length us, event | category | flops | bytes accessed | tf_op | source)
XLA Modules:
  0.0 69.8 jit_solution(14778669938690006390)
XLA Ops:
  0.6 0.0 copy-start
  0.6 0.0 copy-start.3
  0.7 0.0 copy-start.2
  0.7 0.0 copy-start.1
  0.7 0.9 %pack.1 = (f32[16,8,128]{2,1,0:T(8,128)S(1)}, f32[8,128]{1,0:T(8,128)S(1)}) custom-call(f32[8,64]{1,0:T(8,128)} %right.1, f32[8,64]{1,0:T(8,128)} %left.1), custom_call_target="tpu_custom_call" | custom-call | flops 10000000000 | bytes 65536 | tf_op jit(solution)/shard_map/pack/pallas_call | solution.py:246
  1.6 22.0 %all_to_all.18.gathered = f32[16,8,128]{2,1,0:T(8,128)S(1)} all-to-all(f32[16,8,128]{2,1,0:T(8,128)S(1)} %get-tuple-element.29), channel_id=1, replica_groups=mesh['row'=16,'far'=2,'chip'=4,'core'=2] {'far','chip','core'}, dimensions={0} | all-to-all | bytes 131072 | tf_op jit(solution)/shard_map/all_to_all | solution.py:254
  23.6 0.0 copy-done
  23.6 0.0 copy-done.3
  23.6 0.0 copy-done.2
  23.6 0.0 copy-done.1
  23.6 0.4 left_product.1
  24.0 3.5 %collective-permute-start = (bf16[16,1536]{1,0:T(8,128)(2,1)S(1)}, bf16[16,1536]{1,0:T(8,128)(2,1)S(1)}, u32[]{:S(2)}, u32[]{:S(2)}) collective-permute-start(bf16[16,1536]{1,0:T(8,128)(2,1)S(1)} %get-tuple-element.31), channel_id=1, source_target_pairs={{0,0},{1,16},{2,32},{3,48},{4,64},{5,80},{6,96},{7,112},{8,128},{9... | collective-permute-start | bytes 147464 | tf_op jit(solution)/shard_map/ppermute | solution.py:262
  27.6 1.9 %collective-permute-done.turned = bf16[16,1536]{1,0:T(8,128)(2,1)S(1)} collective-permute-done((bf16[16,1536]{1,0:T(8,128)(2,1)S(1)}, bf16[16,1536]{1,0:T(8,128)(2,1)S(1)}, u32[]{:S(2)}, u32[]{:S(2)}) %collective-permute-start) | collective-permute-done | bytes 49184 | tf_op jit(solution)/shard_map/ppermute | solution.py:262
  29.4 0.7 %right_product.1 = f32[272,128]{1,0:T(8,128)S(1)} custom-call(bf16[16,1536]{1,0:T(8,128)(2,1)S(1)} %collective-permute-done.turned, bf16[1024,1024]{1,0:T(8,128)(2,1)S(1)} %copy-done, f32[8,128]{1,0:T(8,128)S(1)} %get-tuple-element.32.damped, f32[1,128]{1,0:T(1,128)S(1)} %get-tuple-element.33.missing), custom_call_target="tpu_custom_call" | custom-call | tf_op jit(solution)/shard_map/right_product/pallas_call | solution.py:264
  30.2 20.8 %all_to_all.19 = f32[16,17,1,128]{3,2,1,0:T(1,128)S(1)} all-to-all(f32[16,17,1,128]{3,2,1,0:T(1,128)S(1)} %bitcast.26), channel_id=1, replica_groups=mesh['row'=16,'far'=2,'chip'=4,'core'=2] {'far','chip','core'}, dimensions={0} | all-to-all | bytes 278528 | tf_op jit(solution)/shard_map/all_to_all | solution.py:269
  51.0 0.3 inner_products.1
  51.3 0.8 %collective-permute-start.1 = (f32[8,128]{1,0:T(8,128)S(1)}, f32[8,128]{1,0:T(8,128)S(1)}, u32[]{:S(2)}, u32[]{:S(2)}) collective-permute-start(f32[8,128]{1,0:T(8,128)S(1)} %get-tuple-element.34), channel_id=1, source_target_pairs={{0,1},{1,0},{2,3},{3,2},{4,5},{5,4},{6,7},{7,6},{8,9},{9,8},{10,11... | collective-permute-start | bytes 12296 | tf_op jit(solution)/shard_map/ppermute | solution.py:276
  52.0 0.8 %collective-permute-done.1 = f32[8,128]{1,0:T(8,128)S(1)} collective-permute-done((f32[8,128]{1,0:T(8,128)S(1)}, f32[8,128]{1,0:T(8,128)S(1)}, u32[]{:S(2)}, u32[]{:S(2)}) %collective-permute-start.1) | collective-permute-done | bytes 4128 | tf_op jit(solution)/shard_map/ppermute | solution.py:276
  52.9 16.0 %all_to_all.20 = f32[64,1,128]{2,1,0:T(1,128)S(1)} all-to-all(f32[64,1,128]{2,1,0:T(1,128)S(1)} %broadcast_in_dim.2), channel_id=1, replica_groups=mesh['row'=16,'far'=2,'chip'=4,'core'=2] {'row','chip'}, dimensions={0} | all-to-all | bytes 65536 | tf_op jit(solution)/shard_map/all_to_all | solution.py:279
  68.9 0.9 %finish.1 = (f32[8,64]{1,0:T(8,128)}, f32[8,64]{1,0:T(8,128)}, f32[3,8]{1,0:T(4,128)}, s32[1,1]{1,0:T(1,128)S(4)}) custom-call(f32[64,128]{1,0:T(8,128)S(1)} %bitcast.28, f32[8,128]{1,0:T(8,128)S(1)} %get-tuple-element.35.reduced, f32[8,128]{1,0:T(8,128)S(1)} %get-tuple-element.30.both), custom_call_target="tpu_custom_call" | custom-call | tf_op jit(solution)/shard_map/finish/pallas_call | solution.py:282
  (4 shorter events, 0.0 us)
Async XLA Ops:
  0.6 23.0 %copy-start = (bf16[1024,1024]{1,0:T(8,128)(2,1)S(1)}, bf16[1024,1024]{1,0:T(8,128)(2,1)}, u32[]{:S(2)}) copy-start(bf16[1024,1024]{1,0:T(8,128)(2,1)} %ladder.3) | copy-start | bytes 6291460
  0.6 22.9 %copy-start.3 = (f32[2,8]{1,0:T(2,128)S(1)}, f32[2,8]{1,0:T(2,128)}, u32[]{:S(2)}) copy-start(f32[2,8]{1,0:T(2,128)} %coupling.1) | copy-start | bytes 196
  0.7 22.9 %copy-start.2 = (f32[8,64]{1,0:T(8,128)S(1)}, f32[8,64]{1,0:T(8,128)}, u32[]{:S(2)}) copy-start(f32[8,64]{1,0:T(8,128)} %prev_left.1) | copy-start | bytes 6148
  0.7 22.9 %copy-start.1 = (f32[8,64]{1,0:T(8,128)S(1)}, f32[8,64]{1,0:T(8,128)}, u32[]{:S(2)}) copy-start(f32[8,64]{1,0:T(8,128)} %prev_right.1) | copy-start | bytes 6148
  24.0 5.4 %collective-permute-start = (bf16[16,1536]{1,0:T(8,128)(2,1)S(1)}, bf16[16,1536]{1,0:T(8,128)(2,1)S(1)}, u32[]{:S(2)}, u32[]{:S(2)}) collective-permute-start(bf16[16,1536]{1,0:T(8,128)(2,1)S(1)} %get-tuple-element.31), channel_id=1, source_target_pairs={{0,0},{1,16},{2,32},{3,48},{4,64},{5,80},{6,96},{7,112},{8,128},{9... | collective-permute-start | bytes 147464 | tf_op jit(solution)/shard_map/ppermute | solution.py:262
  51.3 1.6 %collective-permute-start.1 = (f32[8,128]{1,0:T(8,128)S(1)}, f32[8,128]{1,0:T(8,128)S(1)}, u32[]{:S(2)}, u32[]{:S(2)}) collective-permute-start(f32[8,128]{1,0:T(8,128)S(1)} %get-tuple-element.34), channel_id=1, source_target_pairs={{0,1},{1,0},{2,3},{3,2},{4,5},{5,4},{6,7},{7,6},{8,9},{9,8},{10,11... | collective-permute-start | bytes 12296 | tf_op jit(solution)/shard_map/ppermute | solution.py:276

commit v7 on v6

--- a/solution.py
+++ b/solution.py
@@ -85,13 +85,16 @@
     missing[...] = jnp.sum(spread, axis=0, keepdims=True)
 
 
+def flip_kernel(ladder, damped, flipped):
+    del damped
+    flipped[...] = ladder[...].T
+
+
 def right_kernel(turned, ladder, damped, missing, out):
     low = lane_of((8, LANES)) < HALF
     width = ladder.shape[1]
     block = turned[:, :width][:8]
-    terms = lax.dot_general(
-        block, ladder[...], (((1,), (1,)), ((), ())), preferred_element_type=jnp.float32
-    )
+    terms = jnp.dot(block, ladder[...], preferred_element_type=jnp.float32)
     tiles = []
     for m in range(width // LANES):
         at = LANES * m
@@ -260,11 +263,19 @@
         )(gathered, ladder, both, previous_right, previous_left, coupling)
     transpose = [(i * count + j, j * count + i) for i in range(count) for j in range(count)]
     turned = lax.ppermute(packed, AXES, transpose)
+    with jax.named_scope("flip"):
+        flipped = pl.pallas_call(
+            flip_kernel, out_shape=jax.ShapeDtypeStruct(ladder.shape[::-1], ladder.dtype),
+            in_specs=[VMEM] * 2, out_specs=VMEM, compiler_params=PARAMS,
+            cost_estimate=pl.CostEstimate(
+                flops=1_000_000_000, bytes_accessed=4_194_304, transcendentals=0
+            ),
+        )(ladder, damped)
     with jax.named_scope("right_product"):
         partials = pl.pallas_call(
             right_kernel, out_shape=jax.ShapeDtypeStruct((count * CHUNK, LANES), jnp.float32),
             in_specs=[VMEM] * 4, out_specs=VMEM, compiler_params=PARAMS,
-        )(turned, ladder, damped, missing)
+        )(turned, flipped, damped, missing)
     partials = partials.reshape(count, CHUNK, 1, LANES)
     partials = lax.all_to_all(partials, COL, 0, 0, tiled=True).reshape(count * CHUNK, LANES)
     with jax.named_scope("inner_products"):

time: 70.1 us -> 69.8 us (level)
  transfers between devices with their start and end apart: 2 -> 2, of which waited for: 2 -> 2; matrix products, arithmetic and copies ran while one was open for 0% -> 0% of each run, Pallas kernels for 0% -> 1%
where the time goes in v7:
time: 69.8 us; the launch traced here: 69.6 us
  blocking collectives  58.8 us (84%)
  starting transfers between devices  4.28 us (6%)
  Pallas kernels  3.64 us (5%)
  waiting for transfers between devices  2.05 us (3%)
  between operations  0.73 us (1%)
    all_to_all x1, blocking collectives, local(): gathered = lax.all_to_all(chunks, COL, 0, 0, tiled=True)  22 us
    all_to_all x1, blocking collectives, local(): lax.all_to_all(partials, COL, 0, 0, tiled=True)  20.8 us
    all_to_all x1, blocking collectives, local(): rows = lax.all_to_all(rows, ROW + COL[1:2], 0, 0, tiled=True)  16 us
    ppermute x1, starting transfers between devices, local(): turned = lax.ppermute(packed, AXES, transpose)  3.52 us
  transfers between devices with their start and end apart: 2, of which 2 were waited for; matrix products, arithmetic and copies ran while one was open for 0% of the time, Pallas kernels for 1%

profile of v7, /device:TPU:1, one launch (start us, length us, event | category | flops | bytes accessed | tf_op | source)
XLA Modules:
  0.0 69.6 jit_solution(13298942709521332132)
XLA Ops:
  0.6 0.0 copy-start
  0.6 0.0 copy-start.3
  0.7 0.0 copy-start.2
  0.7 0.0 copy-start.1
  0.7 0.9 %pack.1 = (f32[16,8,128]{2,1,0:T(8,128)S(1)}, f32[8,128]{1,0:T(8,128)S(1)}) custom-call(f32[8,64]{1,0:T(8,128)} %right.1, f32[8,64]{1,0:T(8,128)} %left.1), custom_call_target="tpu_custom_call" | custom-call | flops 10000000000 | bytes 65536 | tf_op jit(solution)/shard_map/pack/pallas_call | solution.py:249
  1.6 22.0 %all_to_all.18.gathered = f32[16,8,128]{2,1,0:T(8,128)S(1)} all-to-all(f32[16,8,128]{2,1,0:T(8,128)S(1)} %get-tuple-element.29), channel_id=1, replica_groups=mesh['row'=16,'far'=2,'chip'=4,'core'=2] {'far','chip','core'}, dimensions={0} | all-to-all | bytes 131072 | tf_op jit(solution)/shard_map/all_to_all | solution.py:257
  23.6 0.0 copy-done
  23.6 0.0 copy-done.3
  23.6 0.0 copy-done.2
  23.6 0.0 copy-done.1
  23.6 0.4 left_product.1
  24.0 3.5 %collective-permute-start = (bf16[16,1536]{1,0:T(8,128)(2,1)S(1)}, bf16[16,1536]{1,0:T(8,128)(2,1)S(1)}, u32[]{:S(2)}, u32[]{:S(2)}) collective-permute-start(bf16[16,1536]{1,0:T(8,128)(2,1)S(1)} %get-tuple-element.31), channel_id=1, source_target_pairs={{0,0},{1,16},{2,32},{3,48},{4,64},{5,80},{6,96},{7,112},{8,128},{9... | collective-permute-start | bytes 147464 | tf_op jit(solution)/shard_map/ppermute | solution.py:265
  27.6 0.6 flip.1.ladder
  28.2 1.2 %collective-permute-done.turned = bf16[16,1536]{1,0:T(8,128)(2,1)S(1)} collective-permute-done((bf16[16,1536]{1,0:T(8,128)(2,1)S(1)}, bf16[16,1536]{1,0:T(8,128)(2,1)S(1)}, u32[]{:S(2)}, u32[]{:S(2)}) %collective-permute-start) | collective-permute-done | bytes 49184 | tf_op jit(solution)/shard_map/ppermute | solution.py:265
  29.4 0.5 right_product.1
  29.9 20.8 %all_to_all.19 = f32[16,17,1,128]{3,2,1,0:T(1,128)S(1)} all-to-all(f32[16,17,1,128]{3,2,1,0:T(1,128)S(1)} %bitcast.26), channel_id=1, replica_groups=mesh['row'=16,'far'=2,'chip'=4,'core'=2] {'far','chip','core'}, dimensions={0} | all-to-all | bytes 278528 | tf_op jit(solution)/shard_map/all_to_all | solution.py:280
  50.7 0.3 inner_products.1
  51.0 0.8 %collective-permute-start.1 = (f32[8,128]{1,0:T(8,128)S(1)}, f32[8,128]{1,0:T(8,128)S(1)}, u32[]{:S(2)}, u32[]{:S(2)}) collective-permute-start(f32[8,128]{1,0:T(8,128)S(1)} %get-tuple-element.34), channel_id=1, source_target_pairs={{0,1},{1,0},{2,3},{3,2},{4,5},{5,4},{6,7},{7,6},{8,9},{9,8},{10,11... | collective-permute-start | bytes 12296 | tf_op jit(solution)/shard_map/ppermute | solution.py:287
  51.8 0.8 %collective-permute-done.1 = f32[8,128]{1,0:T(8,128)S(1)} collective-permute-done((f32[8,128]{1,0:T(8,128)S(1)}, f32[8,128]{1,0:T(8,128)S(1)}, u32[]{:S(2)}, u32[]{:S(2)}) %collective-permute-start.1) | collective-permute-done | bytes 4128 | tf_op jit(solution)/shard_map/ppermute | solution.py:287
  52.6 16.0 %all_to_all.20 = f32[64,1,128]{2,1,0:T(1,128)S(1)} all-to-all(f32[64,1,128]{2,1,0:T(1,128)S(1)} %broadcast_in_dim.2), channel_id=1, replica_groups=mesh['row'=16,'far'=2,'chip'=4,'core'=2] {'row','chip'}, dimensions={0} | all-to-all | bytes 65536 | tf_op jit(solution)/shard_map/all_to_all | solution.py:290
  68.7 0.9 %finish.1 = (f32[8,64]{1,0:T(8,128)}, f32[8,64]{1,0:T(8,128)}, f32[3,8]{1,0:T(4,128)}, s32[1,1]{1,0:T(1,128)S(4)}) custom-call(f32[64,128]{1,0:T(8,128)S(1)} %bitcast.28, f32[8,128]{1,0:T(8,128)S(1)} %get-tuple-element.35.reduced, f32[8,128]{1,0:T(8,128)S(1)} %get-tuple-element.30.both), custom_call_target="tpu_custom_call" | custom-call | tf_op jit(solution)/shard_map/finish/pallas_call | solution.py:293
  (4 shorter events, 0.0 us)
Async XLA Ops:
  0.6 23.0 %copy-start = (bf16[1024,1024]{1,0:T(8,128)(2,1)S(1)}, bf16[1024,1024]{1,0:T(8,128)(2,1)}, u32[]{:S(2)}) copy-start(bf16[1024,1024]{1,0:T(8,128)(2,1)} %ladder.3) | copy-start | bytes 6291460
  0.6 22.9 %copy-start.3 = (f32[2,8]{1,0:T(2,128)S(1)}, f32[2,8]{1,0:T(2,128)}, u32[]{:S(2)}) copy-start(f32[2,8]{1,0:T(2,128)} %coupling.1) | copy-start | bytes 196
  0.7 22.9 %copy-start.2 = (f32[8,64]{1,0:T(8,128)S(1)}, f32[8,64]{1,0:T(8,128)}, u32[]{:S(2)}) copy-start(f32[8,64]{1,0:T(8,128)} %prev_left.1) | copy-start | bytes 6148
  0.7 22.9 %copy-start.1 = (f32[8,64]{1,0:T(8,128)S(1)}, f32[8,64]{1,0:T(8,128)}, u32[]{:S(2)}) copy-start(f32[8,64]{1,0:T(8,128)} %prev_right.1) | copy-start | bytes 6148
  24.0 5.4 %collective-permute-start = (bf16[16,1536]{1,0:T(8,128)(2,1)S(1)}, bf16[16,1536]{1,0:T(8,128)(2,1)S(1)}, u32[]{:S(2)}, u32[]{:S(2)}) collective-permute-start(bf16[16,1536]{1,0:T(8,128)(2,1)S(1)} %get-tuple-element.31), channel_id=1, source_target_pairs={{0,0},{1,16},{2,32},{3,48},{4,64},{5,80},{6,96},{7,112},{8,128},{9... | collective-permute-start | bytes 147464 | tf_op jit(solution)/shard_map/ppermute | solution.py:265
  51.0 1.6 %collective-permute-start.1 = (f32[8,128]{1,0:T(8,128)S(1)}, f32[8,128]{1,0:T(8,128)S(1)}, u32[]{:S(2)}, u32[]{:S(2)}) collective-permute-start(f32[8,128]{1,0:T(8,128)S(1)} %get-tuple-element.34), channel_id=1, source_target_pairs={{0,1},{1,0},{2,3},{3,2},{4,5},{5,4},{6,7},{7,6},{8,9},{9,8},{10,11... | collective-permute-start | bytes 12296 | tf_op jit(solution)/shard_map/ppermute | solution.py:287

commit v8 on v7

--- a/solution.py
+++ b/solution.py
@@ -131,9 +131,12 @@
     for far in range(2):
         pair = gathered[far * half + near]
         crossed = swap(pair)
-        work = partials[8 * far : 8 * far + 8, :]
-        for at in range(1, count):
-            work = work + partials[CHUNK * at + 8 * far : CHUNK * at + 8 * far + 8, :]
+        parts = [
+            partials[CHUNK * at + 8 * far : CHUNK * at + 8 * far + 8, :] for at in range(count)
+        ]
+        while len(parts) > 1:
+            parts = [first + second for first, second in zip(parts[::2], parts[1::2], strict=True)]
+        work = parts[0]
 
         @pl.when(mine == far)
         def _(work=work):
@@ -168,7 +171,7 @@
         table = jnp.where(slot == at, dot, table)
     row = jnp.sum(jnp.where(lane % 8 == sublane_of(shape), table, 0.0), axis=0, keepdims=True)
     row = row + jnp.where(lane[:1] < 8, lack * (1.0 / half), 0.0)
-    rows[...] = jnp.broadcast_to(row, rows.shape)
+    rows[...] = row
 
 
 def finish_kernel(
@@ -281,12 +284,12 @@
     with jax.named_scope("inner_products"):
         rows, reduced = pl.pallas_call(
             products_kernel,
-            out_shape=(tile, tile),
+            out_shape=(jax.ShapeDtypeStruct((1, LANES), jnp.float32), tile),
             in_specs=[VMEM] * 2, out_specs=(VMEM,) * 2, compiler_params=PARAMS,
         )(partials, gathered)
     other = lax.ppermute(rows, "core", ((0, 1), (1, 0)))
     with jax.named_scope("chip_total"):
-        rows = jnp.broadcast_to((rows + other)[:1], (devices // 4, LANES))
+        rows = jnp.broadcast_to(rows + other, (devices // 4, LANES))
     rows = lax.all_to_all(rows, ROW + COL[1:2], 0, 0, tiled=True)
     half_out = pltpu.HBM((8, HALF), jnp.float32)
     with jax.named_scope("finish"):

time: 69.8 us -> 69.8 us (level)
  no operation moved by 1% of the time
where the time goes in v8:
time: 69.8 us; the launch traced here: 69.5 us
  blocking collectives  58.8 us (84%)
  starting transfers between devices  4.28 us (6%)
  Pallas kernels  3.63 us (5%)
  waiting for transfers between devices  2.05 us (3%)
  between operations  0.73 us (1%)
    all_to_all x1, blocking collectives, local(): gathered = lax.all_to_all(chunks, COL, 0, 0, tiled=True)  22 us
    all_to_all x1, blocking collectives, local(): lax.all_to_all(partials, COL, 0, 0, tiled=True)  20.8 us
    all_to_all x1, blocking collectives, local(): rows = lax.all_to_all(rows, ROW + COL[1:2], 0, 0, tiled=True)  16 us
    ppermute x1, starting transfers between devices, local(): turned = lax.ppermute(packed, AXES, transpose)  3.52 us
  transfers between devices with their start and end apart: 2, of which 2 were waited for; matrix products, arithmetic and copies ran while one was open for 0% of the time, Pallas kernels for 1%

profile of v8, /device:TPU:1, one launch (start us, length us, event | category | flops | bytes accessed | tf_op | source)
XLA Modules:
  0.0 69.5 jit_solution(11212424607933145423)
XLA Ops:
  0.6 0.0 copy-start
  0.6 0.0 copy-start.3
  0.7 0.0 copy-start.2
  0.7 0.0 copy-start.1
  0.7 0.9 %pack.1 = (f32[16,8,128]{2,1,0:T(8,128)S(1)}, f32[8,128]{1,0:T(8,128)S(1)}) custom-call(f32[8,64]{1,0:T(8,128)} %right.1, f32[8,64]{1,0:T(8,128)} %left.1), custom_call_target="tpu_custom_call" | custom-call | flops 10000000000 | bytes 65536 | tf_op jit(solution)/shard_map/pack/pallas_call | solution.py:252
  1.6 22.0 %all_to_all.18.gathered = f32[16,8,128]{2,1,0:T(8,128)S(1)} all-to-all(f32[16,8,128]{2,1,0:T(8,128)S(1)} %get-tuple-element.29), channel_id=1, replica_groups=mesh['row'=16,'far'=2,'chip'=4,'core'=2] {'far','chip','core'}, dimensions={0} | all-to-all | bytes 131072 | tf_op jit(solution)/shard_map/all_to_all | solution.py:260
  23.6 0.0 copy-done
  23.6 0.0 copy-done.3
  23.6 0.0 copy-done.2
  23.6 0.0 copy-done.1
  23.6 0.4 left_product.1
  24.0 3.5 %collective-permute-start = (bf16[16,1536]{1,0:T(8,128)(2,1)S(1)}, bf16[16,1536]{1,0:T(8,128)(2,1)S(1)}, u32[]{:S(2)}, u32[]{:S(2)}) collective-permute-start(bf16[16,1536]{1,0:T(8,128)(2,1)S(1)} %get-tuple-element.31), channel_id=1, source_target_pairs={{0,0},{1,16},{2,32},{3,48},{4,64},{5,80},{6,96},{7,112},{8,128},{9... | collective-permute-start | bytes 147464 | tf_op jit(solution)/shard_map/ppermute | solution.py:268
  27.6 0.6 flip.1.ladder
  28.2 1.2 %collective-permute-done.turned = bf16[16,1536]{1,0:T(8,128)(2,1)S(1)} collective-permute-done((bf16[16,1536]{1,0:T(8,128)(2,1)S(1)}, bf16[16,1536]{1,0:T(8,128)(2,1)S(1)}, u32[]{:S(2)}, u32[]{:S(2)}) %collective-permute-start) | collective-permute-done | bytes 49184 | tf_op jit(solution)/shard_map/ppermute | solution.py:268
  29.4 0.5 right_product.1
  29.9 20.8 %all_to_all.19 = f32[16,17,1,128]{3,2,1,0:T(1,128)S(1)} all-to-all(f32[16,17,1,128]{3,2,1,0:T(1,128)S(1)} %bitcast.26), channel_id=1, replica_groups=mesh['row'=16,'far'=2,'chip'=4,'core'=2] {'far','chip','core'}, dimensions={0} | all-to-all | bytes 278528 | tf_op jit(solution)/shard_map/all_to_all | solution.py:283
  50.7 0.3 inner_products.1
  51.0 0.8 %collective-permute-start.1 = (f32[1,128]{1,0:T(1,128)S(1)}, f32[1,128]{1,0:T(1,128)S(1)}, u32[]{:S(2)}, u32[]{:S(2)}) collective-permute-start(f32[1,128]{1,0:T(1,128)S(1)} %get-tuple-element.34), channel_id=1, source_target_pairs={{0,1},{1,0},{2,3},{3,2},{4,5},{5,4},{6,7},{7,6},{8,9},{9,8},{10,11... | collective-permute-start | bytes 1544 | tf_op jit(solution)/shard_map/ppermute | solution.py:290
  51.8 0.8 %collective-permute-done.1 = f32[1,128]{1,0:T(1,128)S(1)} collective-permute-done((f32[1,128]{1,0:T(1,128)S(1)}, f32[1,128]{1,0:T(1,128)S(1)}, u32[]{:S(2)}, u32[]{:S(2)}) %collective-permute-start.1) | collective-permute-done | bytes 544 | tf_op jit(solution)/shard_map/ppermute | solution.py:290
  52.6 16.0 %all_to_all.20 = f32[64,1,128]{2,1,0:T(1,128)S(1)} all-to-all(f32[64,1,128]{2,1,0:T(1,128)S(1)} %broadcast_in_dim.2), channel_id=1, replica_groups=mesh['row'=16,'far'=2,'chip'=4,'core'=2] {'row','chip'}, dimensions={0} | all-to-all | bytes 65536 | tf_op jit(solution)/shard_map/all_to_all | solution.py:293
  68.6 0.9 %finish.1 = (f32[8,64]{1,0:T(8,128)}, f32[8,64]{1,0:T(8,128)}, f32[3,8]{1,0:T(4,128)}, s32[1,1]{1,0:T(1,128)S(4)}) custom-call(f32[64,128]{1,0:T(8,128)S(1)} %bitcast.28, f32[8,128]{1,0:T(8,128)S(1)} %get-tuple-element.35.reduced, f32[8,128]{1,0:T(8,128)S(1)} %get-tuple-element.30.both), custom_call_target="tpu_custom_call" | custom-call | tf_op jit(solution)/shard_map/finish/pallas_call | solution.py:296
  (3 shorter events, 0.0 us)
Async XLA Ops:
  0.6 23.0 %copy-start = (bf16[1024,1024]{1,0:T(8,128)(2,1)S(1)}, bf16[1024,1024]{1,0:T(8,128)(2,1)}, u32[]{:S(2)}) copy-start(bf16[1024,1024]{1,0:T(8,128)(2,1)} %ladder.3) | copy-start | bytes 6291460
  0.6 22.9 %copy-start.3 = (f32[2,8]{1,0:T(2,128)S(1)}, f32[2,8]{1,0:T(2,128)}, u32[]{:S(2)}) copy-start(f32[2,8]{1,0:T(2,128)} %coupling.1) | copy-start | bytes 196
  0.7 22.9 %copy-start.2 = (f32[8,64]{1,0:T(8,128)S(1)}, f32[8,64]{1,0:T(8,128)}, u32[]{:S(2)}) copy-start(f32[8,64]{1,0:T(8,128)} %prev_left.1) | copy-start | bytes 6148
  0.7 22.9 %copy-start.1 = (f32[8,64]{1,0:T(8,128)S(1)}, f32[8,64]{1,0:T(8,128)}, u32[]{:S(2)}) copy-start(f32[8,64]{1,0:T(8,128)} %prev_right.1) | copy-start | bytes 6148
  24.0 5.4 %collective-permute-start = (bf16[16,1536]{1,0:T(8,128)(2,1)S(1)}, bf16[16,1536]{1,0:T(8,128)(2,1)S(1)}, u32[]{:S(2)}, u32[]{:S(2)}) collective-permute-start(bf16[16,1536]{1,0:T(8,128)(2,1)S(1)} %get-tuple-element.31), channel_id=1, source_target_pairs={{0,0},{1,16},{2,32},{3,48},{4,64},{5,80},{6,96},{7,112},{8,128},{9... | collective-permute-start | bytes 147464 | tf_op jit(solution)/shard_map/ppermute | solution.py:268
  51.0 1.6 %collective-permute-start.1 = (f32[1,128]{1,0:T(1,128)S(1)}, f32[1,128]{1,0:T(1,128)S(1)}, u32[]{:S(2)}, u32[]{:S(2)}) collective-permute-start(f32[1,128]{1,0:T(1,128)S(1)} %get-tuple-element.34), channel_id=1, source_target_pairs={{0,1},{1,0},{2,3},{3,2},{4,5},{5,4},{6,7},{7,6},{8,9},{9,8},{10,11... | collective-permute-start | bytes 1544 | tf_op jit(solution)/shard_map/ppermute | solution.py:290
